TPU v7x, 512 devices: a whole 4x8x8 slice. The times are simulated.
512 devices in a mesh: seq: 128 (over z, y, x_hi), ch: 4 (over x_lo, core).
Axes of the slice: x: 4 (x_hi: 2, x_lo: 2; x = x_hi * 2 + x_lo), y: 8, z: 8, core: 2. Of those that a mesh axis runs over, the one named last changes fastest.
Arguments:
- tokens: bfloat16 [32768, 1024], P('seq', 'ch'), may hold values from -24 to 24
- cotangent: bfloat16 [32768, 1024], P('seq', 'ch'), may hold values from -6 to 6
- first_factor: bfloat16 [16, 64, 64], replicated, may hold values from -0.75 to 0.75
- second_factor: bfloat16 [64, 16, 16], replicated, may hold values from -1.5 to 1.5
- third_factor: bfloat16 [64, 32, 32], replicated, may hold values from -1 to 1
- gate_weight: bfloat16 [1024, 1024], P(None, 'ch'), may hold values from -0.1875 to 0.1875
Outputs:
- output: bfloat16 [32768, 1024], P('seq', 'ch')
- input_grad: bfloat16 [32768, 1024], P('seq', 'ch')
- first_grad: bfloat16 [16, 64, 64], replicated
- second_grad: bfloat16 [64, 16, 16], replicated
- third_grad: bfloat16 [64, 32, 32], replicated
- gate_grad: float32 [1024, 1024], P('seq', 'ch')
All inputs are finite; a program needn't handle non-finite values.
Results may differ from a plain program's by a relative error of at most 0.0068.
Values may be sent and summed in bfloat16 or wider, within the bound.
A program may use at most 64 MiB of HBM per device.

v0:
```python
import jax
import jax.numpy as jnp
from jax import lax
from jax.sharding import Mesh
from jax.sharding import PartitionSpec as P

A = 32
B = 16
C = 64
SEQ = ("seq_0", "seq_1", "seq_2")
SEQ_CH = ("seq_0", "seq_1", "seq_2", "ch")


def sent_together(arrays, axis, dim, along):
    both = jnp.concatenate(arrays, axis=along)
    out, at, outs = (lax.all_gather(both, axis, axis=dim, tiled=True), 0, [])
    for a in arrays:
        outs.append(lax.slice_in_dim(out, at, at + a.shape[along], axis=along))
        at += a.shape[along]
    return tuple(outs)


def joined_along(blocks, dim):
    blocks = jnp.moveaxis(blocks, 0, dim)
    lengths = blocks.shape
    return blocks.reshape(*lengths[:dim], lengths[dim] * lengths[dim + 1], *lengths[dim + 2 :])


def sent_to_all(x, axis):
    copies = jnp.broadcast_to(x, (lax.axis_size(axis), *x.shape))
    return lax.all_to_all(copies, axis, split_axis=0, concat_axis=0, tiled=True)


def collect(x, axis, dim):
    return joined_along(sent_to_all(x, axis), dim)


def sum_by_axis(total, axes):
    for axis in axes:
        total = lax.psum_scatter(total, axis, scatter_dimension=0, tiled=True)
    return total


def on_device(tokens, cotangent, first_factor, second_factor, third_factor, gate_weight):
    seq_count = lax.axis_size(SEQ)
    seq_index = lax.axis_index(SEQ)
    per_device_c = max(1, C // seq_count)
    splits = max(1, seq_count // C)
    local_rows, width = tokens.shape
    narrow = width // splits
    blocks = local_rows // C
    batch_b = min(blocks, B)
    start_b = seq_index * blocks % B
    first_sel = lax.dynamic_slice_in_dim(first_factor, start_b, blocks, 0)
    column = seq_index // splits * per_device_c
    second_sel = lax.dynamic_slice_in_dim(second_factor, column, per_device_c, 0)
    third_sel = lax.dynamic_slice_in_dim(third_factor, column, per_device_c, 0)
    grid_view = tokens.reshape(blocks // batch_b, batch_b, C, width)
    mixed_first = jnp.einsum(
        "bcd,ibdh->ibch", first_sel, grid_view, preferred_element_type=jnp.float32
    ).astype(jnp.bfloat16)

    def spread(values):
        return values.reshape(blocks, seq_count, per_device_c, narrow)

    received = lax.all_to_all(spread(mixed_first), SEQ, split_axis=1, concat_axis=0, tiled=True)
    item_count = received.shape[3]
    far_view = received.reshape(A, B, per_device_c, item_count)
    second_val = jnp.einsum(
        "kbe,aekh->abkh", second_sel, far_view, preferred_element_type=jnp.float32
    ).astype(jnp.bfloat16)
    third_val = jnp.einsum(
        "kae,ebkh->abkh", third_sel, second_val, preferred_element_type=jnp.float32
    ).astype(jnp.bfloat16)
    first_far = received
    second_far = second_val.reshape(A * B, 1, per_device_c, item_count)
    mixed_far = third_val.reshape(A * B, 1, per_device_c, item_count)
    mixed_back = lax.all_to_all(mixed_far, SEQ, split_axis=0, concat_axis=1, tiled=True).reshape(
        local_rows, width
    )
    full_tokens, full_weight = sent_together((tokens, gate_weight), "ch", 1, 0)
    own_rows = lax.dynamic_slice_in_dim(full_weight, lax.axis_index("ch") * width, width, 0)
    gate_pre = jnp.dot(full_tokens, gate_weight, preferred_element_type=jnp.float32)
    sigmoid_gate = jax.nn.sigmoid(gate_pre)
    activation = gate_pre * sigmoid_gate
    mixed_float = mixed_back.astype(jnp.float32)
    output = (tokens.astype(jnp.float32) + mixed_float * activation).astype(jnp.bfloat16)
    upstream = cotangent.astype(jnp.float32)
    mix_grad = (upstream * activation).astype(jnp.bfloat16)
    pre_grad = (
        upstream * mixed_float * sigmoid_gate * (1.0 + gate_pre * (1.0 - sigmoid_gate))
    ).astype(jnp.bfloat16)
    received = lax.all_to_all(spread(mix_grad), SEQ, split_axis=1, concat_axis=0, tiled=True)
    item_count = received.shape[3]
    far_view = received.reshape(A, B, per_device_c, item_count)
    back_second = jnp.einsum(
        "kae,abkh->ebkh", third_sel, far_view, preferred_element_type=jnp.float32
    ).astype(jnp.bfloat16)
    back_first = jnp.einsum(
        "kbe,abkh->aekh", second_sel, back_second, preferred_element_type=jnp.float32
    ).astype(jnp.bfloat16)
    second_back = back_second.reshape(A * B, 1, per_device_c, item_count)
    first_back = back_first.reshape(A * B, 1, per_device_c, item_count)
    third_part = jnp.einsum(
        "abkh,ebkh->kae",
        received.reshape(A, B, per_device_c, narrow),
        second_far.reshape(A, B, per_device_c, narrow),
        preferred_element_type=jnp.float32,
    )
    second_part = jnp.einsum(
        "abkh,aekh->kbe",
        second_back.reshape(A, B, per_device_c, narrow),
        first_far.reshape(A, B, per_device_c, narrow),
        preferred_element_type=jnp.float32,
    )
    first_home = lax.all_to_all(first_back, SEQ, split_axis=0, concat_axis=1, tiled=True).reshape(
        blocks // batch_b, batch_b, C, width
    )
    mix_input = jnp.einsum(
        "bcd,ibch->ibdh", first_sel, first_home, preferred_element_type=jnp.float32
    ).reshape(local_rows, width)
    first_part = jnp.einsum(
        "ibch,ibdh->bcd", first_home, grid_view, preferred_element_type=jnp.float32
    )
    first_full = lax.dynamic_update_slice_in_dim(
        jnp.zeros((B, C, C), jnp.float32), first_part, start_b, 0
    )
    second_full = lax.dynamic_update_slice_in_dim(
        jnp.zeros((C, B, B), jnp.float32), second_part, column, 0
    )
    third_full = lax.dynamic_update_slice_in_dim(
        jnp.zeros((C, A, A), jnp.float32), third_part, column, 0
    )
    first_sum, second_sum, third_sum = lax.psum((first_full, second_full, third_full), SEQ_CH)
    gate_input = lax.dot_general(
        collect(pre_grad, "ch", 1),
        own_rows,
        (((1,), (1,)), ((), ())),
        preferred_element_type=jnp.float32,
    )
    gate_grad = sum_by_axis(
        lax.dot_general(
            full_tokens, pre_grad, (((0,), (0,)), ((), ())), preferred_element_type=jnp.float32
        ),
        SEQ,
    )
    input_grad = (upstream + mix_input + gate_input).astype(jnp.bfloat16)
    return (
        output,
        input_grad,
        first_sum.astype(jnp.bfloat16),
        second_sum.astype(jnp.bfloat16),
        third_sum.astype(jnp.bfloat16),
        gate_grad,
    )


def solution(mesh):
    torus = Mesh(mesh.devices.reshape(8, 8, 2, mesh.shape["ch"]), ("seq_0", "seq_1", "seq_2", "ch"))
    return jax.shard_map(
        on_device,
        mesh=torus,
        in_specs=(P(SEQ, "ch"), P(SEQ, "ch"), P(), P(), P(), P(None, "ch")),
        out_specs=(P(SEQ, "ch"), P(SEQ, "ch"), P(), P(), P(), P(SEQ, "ch")),
        check_vma=False,
    )
```

profile of v0, /device:TPU:1, one launch (start us, length us, event | category | flops | bytes accessed | tf_op | source)
XLA Modules:
  0.0 269.6 jit_solution(11293705541648885090)
XLA Ops:
  7.3 2.0 pad_maximum_fusion
  9.6 0.8 copy.64
  10.3 20.8 %all-to-all-start = ((bf16[4,128,1,128]{3,0,2,1:T(4,128)(2,1)}), bf16[4,128,1,128]{3,0,2,1:T(4,128)(2,1)S(1)}, u32[]{:S(2)}, u32[]{:S(2)}) async-start(bf16[4,128,1,128]{3,0,2,1:T(4,128)(2,1)} %copy.64), calls=%async_computation | async-start | bytes 262144 | tf_op jit(solution)/shard_map/all_to_all | solution.py:66
  31.9 11.8 %all-to-all-done = bf16[4,128,1,128]{3,0,2,1:T(4,128)(2,1)S(1)} async-done(((bf16[4,128,1,128]{3,0,2,1:T(4,128)(2,1)}), bf16[4,128,1,128]{3,0,2,1:T(4,128)(2,1)S(1)}, u32[]{:S(2)}, u32[]{:S(2)}) %all-to-all-start) | async-done | bytes 131104 | tf_op jit(solution)/shard_map/all_to_all | solution.py:66
  44.6 0.7 reduce
  45.4 18.1 %all_to_all.59 = bf16[128,2,256]{2,1,0:T(2,128)(2,1)S(1)} all-to-all(bf16[128,2,256]{2,1,0:T(2,128)(2,1)S(1)} %reshape.120), channel_id=1, replica_groups=mesh['seq_0'=8,'seq_1'=8,'seq_2'=2,'ch'=4] {'seq_0','seq_1','seq_2'}, dimensions={0} | all-to-all | bytes 262144 | tf_op jit(solution)/shard_map/all_to_all | solution.py:78
  63.7 0.8 reshape.112
  64.5 2.4 fusion.13
  66.9 0.7 copy-done.11
  67.5 1.3 fusion.6
  68.9 0.8 copy.72
  69.7 8.5 %all-to-all-start.2 = ((bf16[4,128,1,128]{3,0,2,1:T(4,128)(2,1)}), bf16[4,128,1,128]{3,0,2,1:T(4,128)(2,1)S(1)}, u32[]{:S(2)}, u32[]{:S(2)}) async-start(bf16[4,128,1,128]{3,0,2,1:T(4,128)(2,1)} %copy.72), calls=%async_computation.2 | async-start | bytes 262144 | tf_op jit(solution)/shard_map/all_to_all | solution.py:93
  78.2 1.7 copy.80
  79.8 10.8 %all-to-all-done.2 = bf16[4,128,1,128]{3,0,2,1:T(4,128)(2,1)S(1)} async-done(((bf16[4,128,1,128]{3,0,2,1:T(4,128)(2,1)}), bf16[4,128,1,128]{3,0,2,1:T(4,128)(2,1)S(1)}, u32[]{:S(2)}, u32[]{:S(2)}) %all-to-all-start.2) | async-done | bytes 131104 | tf_op jit(solution)/shard_map/all_to_all | solution.py:93
  91.2 0.7 reduce.1
  91.8 0.7 reshape.122
  92.6 6.2 %all-to-all-start.3 = ((bf16[128,2,256]{2,1,0:T(2,128)(2,1)}), bf16[128,2,256]{2,1,0:T(2,128)(2,1)S(1)}, u32[]{:S(2)}, u32[]{:S(2)}) async-start(bf16[128,2,256]{2,1,0:T(2,128)(2,1)} %reshape.122), calls=%async_computation.3 | async-start | bytes 262144 | tf_op jit(solution)/shard_map/all_to_all | solution.py:116
  100.5 0.8 dynamic_update_slice.11
  101.3 10.0 %all-to-all-done.3 = bf16[128,2,256]{2,1,0:T(2,128)(2,1)S(1)} async-done(((bf16[128,2,256]{2,1,0:T(2,128)(2,1)}), bf16[128,2,256]{2,1,0:T(2,128)(2,1)S(1)}, u32[]{:S(2)}, u32[]{:S(2)}) %all-to-all-start.3) | async-done | bytes 131104 | tf_op jit(solution)/shard_map/all_to_all | solution.py:116
  111.3 0.7 copy-done.4
  111.9 0.8 broadcast_in_dim.12
  112.8 7.2 %all-to-all-start.4 = ((bf16[4,256,256]{1,2,0:T(8,128)(2,1)}), bf16[4,256,256]{1,2,0:T(8,128)(2,1)S(1)}, u32[]{:S(2)}, u32[]{:S(2)}) async-start(bf16[4,256,256]{1,2,0:T(8,128)(2,1)} %broadcast_in_dim.12), calls=%async_computation.4 | async-start | bytes 1048576 | tf_op jit(solution)/shard_map/all_to_all | solution.py:31
  120.0 2.0 reshape.123
  121.9 1.0 copy.91
  122.9 0.7 copy.78
  123.6 1.6 reshape.109
  125.2 1.8 fusion.21
  127.1 0.9 broadcast_in_dim.13
  127.9 1.7 convolution_dynamic-update-slice_fusion
  129.7 2.0 fusion
  131.7 21.5 %reduce-scatter.6.cloned.1.call-done = f32[16,256]{1,0:T(8,128)} async-done(((f32[128,256]{1,0:T(8,128)}), f32[16,256]{1,0:T(8,128)}) %reduce-scatter.6.cloned.1.call-update) | async-done | bytes 16400 | tf_op jit(solution)/shard_map/reduce_scatter | solution.py:40
  153.2 109.8 %all-reduce.2 = (bf16[16,64,64]{2,1,0:T(8,128)(2,1)}, bf16[64,16,16]{0,2,1:T(8,128)(2,1)}, bf16[64,32,32]{0,2,1:T(8,128)(2,1)}) all-reduce(f32[16,64,64]{2,1,0:T(8,128)} %convolution_dynamic-update-slice_fusion, f32[64,16,16]{0,2,1:T(8,128)} %copy-done.5, ...), channel_id=1, replica_groups=mesh['seq_0'=8,'seq_1'=8,'seq_2'=2,'ch'=4] {'seq_0','seq_1','seq_2','ch'}, use_global_device_ids=true, to_apply=%region_0.1 | all-reduce | flops 147456 | bytes 884736 | tf_op jit(solution)/shard_map/psum | solution.py:134
  (67 shorter events, 4.4 us)
Async XLA Ops:
  7.2 2.2 copy-start
  7.2 2.2 copy-start.2
  7.2 24.0 %copy-start.14 = (bf16[64,16,16]{0,2,1:T(8,128)(2,1)S(1)}, bf16[64,16,16]{0,2,1:T(8,128)(2,1)}, u32[]{:S(2)}) copy-start(bf16[64,16,16]{0,2,1:T(8,128)(2,1)} %param.9) | copy-start | bytes 98308
  7.2 24.3 %copy-start.12 = (bf16[64,32,32]{0,2,1:T(8,128)(2,1)S(1)}, bf16[64,32,32]{0,2,1:T(8,128)(2,1)}, u32[]{:S(2)}) copy-start(bf16[64,32,32]{0,2,1:T(8,128)(2,1)} %param.10) | copy-start | bytes 393220
  7.2 57.2 %all-gather.2.cloned.1.call-start = ((), (), s32[]{:S(2)}) async-start(), calls=%async_computation.8 | async-start | bytes 3276800 | tf_op jit(solution)/shard_map/all_gather | solution.py:16
  10.3 33.4 %all-to-all-start = ((bf16[4,128,1,128]{3,0,2,1:T(4,128)(2,1)}), bf16[4,128,1,128]{3,0,2,1:T(4,128)(2,1)S(1)}, u32[]{:S(2)}, u32[]{:S(2)}) async-start(bf16[4,128,1,128]{3,0,2,1:T(4,128)(2,1)} %copy.64), calls=%async_computation | async-start | bytes 262144 | tf_op jit(solution)/shard_map/all_to_all | solution.py:66
  31.2 95.9 %reduce-scatter.4.cloned.1.call-start = ((), (), s32[]{:S(2)}) async-start(), calls=%async_computation.9 | async-start | bytes 1179648 | tf_op jit(solution)/shard_map/reduce_scatter | solution.py:40
  31.7 32.8 %copy-start.6 = (bf16[1024,256]{1,0:T(8,128)(2,1)S(1)}, bf16[1024,256]{1,0:T(8,128)(2,1)}, u32[]{:S(2)}) copy-start(bf16[1024,256]{1,0:T(8,128)(2,1)} %param.11) | copy-start | bytes 1572868
  43.7 1.6 copy-start.7
  43.8 20.6 %copy-start.9 = (bf16[32,16,128]{2,1,0:T(8,128)(2,1)}, bf16[32,16,128]{2,1,0:T(8,128)(2,1)S(1)}, u32[]{:S(2)}) copy-start(bf16[32,16,128]{2,1,0:T(8,128)(2,1)S(1)} %fusion.3) | copy-start | bytes 393220
  64.5 3.1 %copy-start.1 = (bf16[1280,1024]{1,0:T(8,128)(2,1)S(1)}, bf16[1280,1024]{1,0:T(8,128)(2,1)}, u32[]{:S(2)}) copy-start(bf16[1280,1024]{1,0:T(8,128)(2,1)} %all-gather.2.cloned.1.call-done) | copy-start | bytes 7864324
  66.9 0.7 copy-start.11
  66.9 2.0 copy-start.13
  69.7 21.0 %all-to-all-start.2 = ((bf16[4,128,1,128]{3,0,2,1:T(4,128)(2,1)}), bf16[4,128,1,128]{3,0,2,1:T(4,128)(2,1)S(1)}, u32[]{:S(2)}, u32[]{:S(2)}) async-start(bf16[4,128,1,128]{3,0,2,1:T(4,128)(2,1)} %copy.72), calls=%async_computation.2 | async-start | bytes 262144 | tf_op jit(solution)/shard_map/all_to_all | solution.py:93
  79.8 18.9 %copy-start.8 = (bf16[4,128,1,128]{3,0,2,1:T(4,128)(2,1)S(1)}, bf16[4,128,1,128]{3,0,2,1:T(4,128)(2,1)}, u32[]{:S(2)}) copy-start(bf16[4,128,1,128]{3,0,2,1:T(4,128)(2,1)} %copy-done.7) | copy-start | bytes 393220
  79.8 20.1 %copy-start.10 = (bf16[32,16,128]{2,1,0:T(8,128)(2,1)S(1)}, bf16[32,16,128]{2,1,0:T(8,128)(2,1)}, u32[]{:S(2)}) copy-start(bf16[32,16,128]{2,1,0:T(8,128)(2,1)} %copy-done.9) | copy-start | bytes 393220
  90.9 21.0 %copy-start.3 = (bf16[256,256]{0,1:T(8,128)(2,1)S(1)}, bf16[256,256]{0,1:T(8,128)(2,1)}, u32[]{:S(2)}) copy-start(bf16[256,256]{0,1:T(8,128)(2,1)} %copy.80) | copy-start | bytes 393220
  92.6 18.7 %all-to-all-start.3 = ((bf16[128,2,256]{2,1,0:T(2,128)(2,1)}), bf16[128,2,256]{2,1,0:T(2,128)(2,1)S(1)}, u32[]{:S(2)}, u32[]{:S(2)}) async-start(bf16[128,2,256]{2,1,0:T(2,128)(2,1)} %reshape.122), calls=%async_computation.3 | async-start | bytes 262144 | tf_op jit(solution)/shard_map/all_to_all | solution.py:116
  99.3 0.7 copy-start.5
  111.3 0.7 copy-start.4
  112.8 16.9 %slice-start = ((bf16[1280,1024]{1,0:T(8,128)(2,1)}), bf16[1024,1024]{1,0:T(8,128)(2,1)S(1)}, s32[]{:S(2)}) async-start(bf16[1280,1024]{1,0:T(8,128)(2,1)} %all-gather.2.cloned.1.call-done), calls=%async_computation.12 | async-start | bytes 4194304 | tf_op jit(solution)/shard_map/slice | solution.py:18
  112.8 16.9 %all-to-all-start.4 = ((bf16[4,256,256]{1,2,0:T(8,128)(2,1)}), bf16[4,256,256]{1,2,0:T(8,128)(2,1)S(1)}, u32[]{:S(2)}, u32[]{:S(2)}) async-start(bf16[4,256,256]{1,2,0:T(8,128)(2,1)} %broadcast_in_dim.12), calls=%async_computation.4 | async-start | bytes 1048576 | tf_op jit(solution)/shard_map/all_to_all | solution.py:31
  120.0 33.2 %reduce-scatter.6.cloned.1.call-start = ((), (), s32[]{:S(2)}) async-start(), calls=%async_computation.10 | async-start | bytes 147456 | tf_op jit(solution)/shard_map/reduce_scatter | solution.py:40
  127.0 136.0 %reduce-scatter.8.cloned.1.call-start = ((), (), s32[]{:S(2)}) async-start(), calls=%async_computation.11 | async-start | bytes 24576 | tf_op jit(solution)/shard_map/reduce_scatter | solution.py:40
Sparse Core Ops, SparseCore 0:
  10.1 46.4 all-gather.1
  69.0 30.8 reduce-scatter.3
  127.2 25.9 reduce-scatter.5
  156.5 23.1 reduce-scatter.7
where the time goes:
time: 270 us
  blocking collectives  128 us (47%)
  waiting for transfers between devices  54.2 us (20%)
  starting transfers between devices  42.8 us (16%)
  local copies, waits for them, and re-layouts  16.6 us (6%)
  between operations  14.1 us (5%)
  matrix products  10.5 us (4%)
  other arithmetic  3.4 us (1%)
    psum x1, blocking collectives, on_device(): lax.psum((first_full, second_full, third_full), SEQ_CH)  110 us
    reduce_scatter x3, waiting for transfers between devices, sum_by_axis(): total = lax.psum_scatter(total, axis, scatter_dimension=0, tiled=True)  21.5 us
    all_to_all x1, starting transfers between devices, on_device(): lax.all_to_all(spread(mixed_first), SEQ, split_axis=1, concat_axis=0, til...  20.8 us
    all_to_all x1, blocking collectives, on_device(): lax.all_to_all(mixed_far, SEQ, split_axis=0, concat_axis=1, tiled=True)  18.1 us
    all_to_all x1, waiting for transfers between devices, on_device(): lax.all_to_all(spread(mixed_first), SEQ, split_axis=1, concat_axis=0, til...  11.8 us
    all_to_all x1, waiting for transfers between devices, on_device(): lax.all_to_all(spread(mix_grad), SEQ, split_axis=1, concat_axis=0, tiled=...  10.8 us
    all_to_all x1, waiting for transfers between devices, on_device(): lax.all_to_all(first_back, SEQ, split_axis=0, concat_axis=1, tiled=True)  10 us
    all_to_all x1, starting transfers between devices, on_device(): lax.all_to_all(spread(mix_grad), SEQ, split_axis=1, concat_axis=0, tiled=...  8.47 us
  transfers between devices with their start and end apart: 8, of which 4 were waited for; matrix products, arithmetic and copies ran while one was open for 8% of the time, Pallas kernels for 0%

commit v1 on v0

--- a/solution.py
+++ b/solution.py
@@ -3,12 +3,64 @@
 from jax import lax
 from jax.sharding import Mesh
 from jax.sharding import PartitionSpec as P
+from jax.experimental import pallas as pl
+from jax.experimental.pallas import tpu as pltpu
 
 A = 32
 B = 16
 C = 64
 SEQ = ("seq_0", "seq_1", "seq_2")
 SEQ_CH = ("seq_0", "seq_1", "seq_2", "ch")
+
+
+def seq_peer(step):
+    me = lax.axis_index(SEQ)
+    peer = lax.rem(me + step, 128)
+    where = {"seq_0": peer // 16, "seq_1": lax.rem(peer // 2, 8), "seq_2": lax.rem(peer, 2)}
+    return me, peer, where
+
+
+def exchange_kernel(x_ref, out_ref, send_sem, recv_sem):
+    barrier = pltpu.get_barrier_semaphore()
+
+    def greet(step, carry):
+        pl.semaphore_signal(
+            barrier, inc=1, device_id=seq_peer(step)[2], device_id_type=pl.DeviceIdType.MESH
+        )
+        return carry
+
+    lax.fori_loop(1, 128, greet, 0)
+    me = lax.axis_index(SEQ)
+    out_ref[pl.ds(me, 1)] = x_ref[pl.ds(me, 1)]
+    pl.semaphore_wait(barrier, 127)
+
+    def send(step, carry):
+        me, peer, where = seq_peer(step)
+        pltpu.make_async_remote_copy(
+            x_ref.at[peer],
+            out_ref.at[me],
+            send_sem,
+            recv_sem,
+            device_id=where,
+            device_id_type=pl.DeviceIdType.MESH,
+        ).start()
+        return carry
+
+    lax.fori_loop(1, 128, send, 0)
+    part = out_ref.at[pl.ds(0, 127)]
+    pltpu.make_async_copy(part, part, send_sem).wait()
+    pltpu.make_async_copy(part, part, recv_sem).wait()
+
+
+def exchange(x):
+    return pl.pallas_call(
+        exchange_kernel,
+        out_shape=jax.ShapeDtypeStruct(x.shape, x.dtype),
+        in_specs=[pl.BlockSpec(memory_space=pltpu.VMEM)],
+        out_specs=pl.BlockSpec(memory_space=pltpu.VMEM),
+        scratch_shapes=[pltpu.SemaphoreType.DMA, pltpu.SemaphoreType.DMA],
+        compiler_params=pltpu.CompilerParams(collective_id=0, has_side_effects=True),
+    )(x)
 
 
 def sent_together(arrays, axis, dim, along):
@@ -61,10 +113,13 @@
     ).astype(jnp.bfloat16)
 
     def spread(values):
-        return values.reshape(blocks, seq_count, per_device_c, narrow)
-
-    received = lax.all_to_all(spread(mixed_first), SEQ, split_axis=1, concat_axis=0, tiled=True)
-    item_count = received.shape[3]
+        return jnp.swapaxes(values.reshape(blocks, seq_count, narrow), 0, 1)
+
+    def home(values):
+        return jnp.swapaxes(exchange(values.reshape(seq_count, blocks, narrow)), 0, 1)
+
+    received = exchange(spread(mixed_first))
+    item_count = received.shape[2]
     far_view = received.reshape(A, B, per_device_c, item_count)
     second_val = jnp.einsum(
         "kbe,aekh->abkh", second_sel, far_view, preferred_element_type=jnp.float32
@@ -75,7 +130,7 @@
     first_far = received
     second_far = second_val.reshape(A * B, 1, per_device_c, item_count)
     mixed_far = third_val.reshape(A * B, 1, per_device_c, item_count)
-    mixed_back = lax.all_to_all(mixed_far, SEQ, split_axis=0, concat_axis=1, tiled=True).reshape(
+    mixed_back = home(mixed_far).reshape(
         local_rows, width
     )
     full_tokens, full_weight = sent_together((tokens, gate_weight), "ch", 1, 0)
@@ -90,8 +145,8 @@
     pre_grad = (
         upstream * mixed_float * sigmoid_gate * (1.0 + gate_pre * (1.0 - sigmoid_gate))
     ).astype(jnp.bfloat16)
-    received = lax.all_to_all(spread(mix_grad), SEQ, split_axis=1, concat_axis=0, tiled=True)
-    item_count = received.shape[3]
+    received = exchange(spread(mix_grad))
+    item_count = received.shape[2]
     far_view = received.reshape(A, B, per_device_c, item_count)
     back_second = jnp.einsum(
         "kae,abkh->ebkh", third_sel, far_view, preferred_element_type=jnp.float32
@@ -113,7 +168,7 @@
         first_far.reshape(A, B, per_device_c, narrow),
         preferred_element_type=jnp.float32,
     )
-    first_home = lax.all_to_all(first_back, SEQ, split_axis=0, concat_axis=1, tiled=True).reshape(
+    first_home = home(first_back).reshape(
         blocks // batch_b, batch_b, C, width
     )
     mix_input = jnp.einsum(

time: 270 us -> 248 us (0.919)
  Pallas kernels: 0 us -> 84.3 us
  waiting for transfers between devices: 54.2 us -> 12.3 us
  starting transfers between devices: 42.8 us -> 7.16 us
  blocking collectives: 128 us -> 108 us
  local copies, waits for them, and re-layouts: 16.6 us -> 8.28 us
    pallas_call x0 -> x4, Pallas kernels: none -> 84.3 us  [exchange(): pl.pallas_call(exchange_kernel, out_shape=jax.ShapeDtypeStruct(x.shape, x...]
    all_to_all x3 -> x0, starting transfers between devices: 35.5 us -> none  [the longest x1 20.8 us: on_device(): lax.all_to_all(spread(mixed_first), SEQ, split_axis=1, concat_axis=0, til...]
    all_to_all x3 -> x0, waiting for transfers between devices: 32.6 us -> none  [the longest x1 11.8 us: on_device(): lax.all_to_all(spread(mixed_first), SEQ, split_axis=1, concat_axis=0, til...]
    all_to_all x1 -> x0, blocking collectives: 18.1 us -> none  [on_device(): lax.all_to_all(mixed_far, SEQ, split_axis=0, concat_axis=1, tiled=True)]
    reduce_scatter x3, waiting for transfers between devices: 21.5 us -> 12.2 us  [sum_by_axis(): total = lax.psum_scatter(total, axis, scatter_dimension=0, tiled=True)]
    unnamed x37 -> x16, local copies, waits for them, and re-layouts: 6.28 us -> 0.46 us
  transfers between devices with their start and end apart: 8 -> 5, of which waited for: 4 -> 1; matrix products, arithmetic and copies ran while one was open for 8% -> 6% of each run, Pallas kernels for 0% -> 34%
where the time goes in v1:
time: 248 us
  blocking collectives  108 us (44%)
  Pallas kernels  84.3 us (34%)
  between operations  14.1 us (6%)
  waiting for transfers between devices  12.3 us (5%)
  matrix products  10.6 us (4%)
  local copies, waits for them, and re-layouts  8.28 us (3%)
  starting transfers between devices  7.16 us (3%)
  other arithmetic  2.95 us (1%)
    psum x1, blocking collectives, on_device(): lax.psum((first_full, second_full, third_full), SEQ_CH)  108 us
    pallas_call x4, Pallas kernels, exchange(): pl.pallas_call(exchange_kernel, out_shape=jax.ShapeDtypeStruct(x.shape, x...  84.3 us
    reduce_scatter x3, waiting for transfers between devices, sum_by_axis(): total = lax.psum_scatter(total, axis, scatter_dimension=0, tiled=True)  12.2 us
    all_to_all x1, starting transfers between devices, sent_to_all(): return lax.all_to_all(copies, axis, split_axis=0, concat_axis=0, tiled=True)  7.04 us
  transfers between devices with their start and end apart: 5, of which 1 were waited for; matrix products, arithmetic and copies ran while one was open for 6% of the time, Pallas kernels for 34%

profile of v1, /device:TPU:1, one launch (start us, length us, event | category | flops | bytes accessed | tf_op | source)
XLA Modules:
  0.0 247.8 jit_solution(16547317295888716996)
XLA Ops:
  7.3 2.0 pad_maximum_fusion
  9.4 0.2 fusion.1
  9.6 0.8 copy.65
  10.4 27.2 %shard_map.109 = bf16[128,4,128]{2,1,0:T(4,128)(2,1)} custom-call(bf16[128,4,128]{2,1,0:T(4,128)(2,1)} %bitcast.89), custom_call_target="tpu_custom_call" | custom-call | tf_op jit(solution)/shard_map/pallas_call | solution.py:56
  37.8 0.2 copy.49
  38.1 0.3 copy.48
  38.3 1.1 fusion.3
  39.4 0.2 fusion.4
  39.6 0.7 copy.28
  40.3 18.8 %shard_map.110 = bf16[128,4,128]{2,1,0:T(4,128)(2,1)} custom-call(bf16[128,4,128]{2,1,0:T(4,128)(2,1)} %bitcast.90), custom_call_target="tpu_custom_call" | custom-call | tf_op jit(solution)/shard_map/pallas_call | solution.py:56
  59.1 0.9 convert_bitcast_fusion
  60.2 2.1 fusion.13
  62.3 2.4 fusion.6
  64.8 0.8 broadcast_in_dim.12
  65.6 7.0 %all-to-all-start = ((bf16[4,256,256]{1,2,0:T(8,128)(2,1)}), bf16[4,256,256]{1,2,0:T(8,128)(2,1)S(1)}, u32[]{:S(2)}, u32[]{:S(2)}) async-start(bf16[4,256,256]{1,2,0:T(8,128)(2,1)} %broadcast_in_dim.12), calls=%async_computation | async-start | bytes 1048576 | tf_op jit(solution)/shard_map/all_to_all | solution.py:83
  72.7 0.8 copy.64
  73.5 19.1 %shard_map.111 = bf16[128,4,128]{2,1,0:T(4,128)(2,1)} custom-call(bf16[128,4,128]{2,1,0:T(4,128)(2,1)} %bitcast.91), custom_call_target="tpu_custom_call" | custom-call | tf_op jit(solution)/shard_map/pallas_call | solution.py:56
  92.7 1.1 fusion.2
  93.8 0.9 convolution_convert_fusion.2
  94.7 19.2 %shard_map.112 = bf16[128,4,128]{2,1,0:T(4,128)(2,1)} custom-call(bf16[128,4,128]{2,1,0:T(4,128)(2,1)} %bitcast.92), custom_call_target="tpu_custom_call" | custom-call | tf_op jit(solution)/shard_map/pallas_call | solution.py:56
  113.8 0.9 copy.35
  114.8 1.1 convolution_bitcast_fusion
  115.9 0.2 convolution_dynamic-update-slice_fusion
  116.1 0.2 convolution_bitcast_fusion.1
  116.3 0.2 copy.39
  116.7 0.3 copy.42
  117.0 0.8 dynamic_update_slice.11
  117.9 108.1 %all-reduce.2 = (bf16[16,64,64]{2,1,0:T(8,128)(2,1)}, bf16[64,16,16]{0,2,1:T(8,128)(2,1)}, bf16[64,32,32]{0,2,1:T(8,128)(2,1)}) all-reduce(f32[16,64,64]{2,1,0:T(8,128)S(1)} %convolution_dynamic-update-slice_fusion, ...), channel_id=1, replica_groups=mesh['seq_0'=8,'seq_1'=8,'seq_2'=2,'ch'=4] {'seq_0','seq_1','seq_2','ch'}, use_global_device_ids=true, to_apply=%region_0.1 | all-reduce | flops 147456 | bytes 884736 | tf_op jit(solution)/shard_map/psum | solution.py:189
  226.0 1.8 slice.9
  227.8 0.2 fusion.21
  228.1 1.0 fusion
  229.1 12.1 %reduce-scatter.8.cloned.1.call-done = f32[8,256]{1,0:T(8,128)} async-done(((f32[16,256]{1,0:T(8,128)}), f32[8,256]{1,0:T(8,128)}) %reduce-scatter.8.cloned.1.call-update) | async-done | bytes 8208 | tf_op jit(solution)/shard_map/reduce_scatter | solution.py:92
  (38 shorter events, 1.1 us)
Async XLA Ops:
  7.2 2.2 copy-start
  7.2 2.2 copy-start.1
  7.2 30.5 %copy-start.6 = (bf16[64,16,16]{0,2,1:T(8,128)(2,1)S(1)}, bf16[64,16,16]{0,2,1:T(8,128)(2,1)}, u32[]{:S(2)}) copy-start(bf16[64,16,16]{0,2,1:T(8,128)(2,1)} %param.9) | copy-start | bytes 98308
  7.2 30.7 %copy-start.4 = (bf16[64,32,32]{0,2,1:T(8,128)(2,1)S(1)}, bf16[64,32,32]{0,2,1:T(8,128)(2,1)}, u32[]{:S(2)}) copy-start(bf16[64,32,32]{0,2,1:T(8,128)(2,1)} %param.10) | copy-start | bytes 393220
  7.2 52.9 %all-gather.2.cloned.1.call-start = ((), (), s32[]{:S(2)}) async-start(), calls=%async_computation.4 | async-start | bytes 3276800 | tf_op jit(solution)/shard_map/all_gather | solution.py:68
  9.3 108.5 %reduce-scatter.4.cloned.1.call-start = ((), (), s32[]{:S(2)}) async-start(), calls=%async_computation.5 | async-start | bytes 1179648 | tf_op jit(solution)/shard_map/reduce_scatter | solution.py:92
  9.6 50.6 %copy-start.2 = (bf16[1024,256]{1,0:T(8,128)(2,1)S(1)}, bf16[1024,256]{1,0:T(8,128)(2,1)}, u32[]{:S(2)}) copy-start(bf16[1024,256]{1,0:T(8,128)(2,1)} %param.11) | copy-start | bytes 1572868
  9.6 50.6 %copy-start.5 = (bf16[256,256]{1,0:T(8,128)(2,1)S(1)}, bf16[256,256]{1,0:T(8,128)(2,1)}, u32[]{:S(2)}) copy-start(bf16[256,256]{1,0:T(8,128)(2,1)} %param.7) | copy-start | bytes 393220
  65.6 50.5 %copy-start.3 = (bf16[128,4,128]{2,1,0:T(4,128)(2,1)S(1)}, bf16[128,4,128]{2,1,0:T(4,128)(2,1)}, u32[]{:S(2)}) copy-start(bf16[128,4,128]{2,1,0:T(4,128)(2,1)} %shard_map.109) | copy-start | bytes 393220
  65.6 162.4 %all-to-all-start = ((bf16[4,256,256]{1,2,0:T(8,128)(2,1)}), bf16[4,256,256]{1,2,0:T(8,128)(2,1)S(1)}, u32[]{:S(2)}, u32[]{:S(2)}) async-start(bf16[4,256,256]{1,2,0:T(8,128)(2,1)} %broadcast_in_dim.12), calls=%async_computation | async-start | bytes 1048576 | tf_op jit(solution)/shard_map/all_to_all | solution.py:83
  72.7 155.4 %reduce-scatter.6.cloned.1.call-start = ((), (), s32[]{:S(2)}) async-start(), calls=%async_computation.6 | async-start | bytes 147456 | tf_op jit(solution)/shard_map/reduce_scatter | solution.py:92
  117.8 123.4 %reduce-scatter.8.cloned.1.call-start = ((), (), s32[]{:S(2)}) async-start(), calls=%async_computation.7 | async-start | bytes 24576 | tf_op jit(solution)/shard_map/reduce_scatter | solution.py:92
Sparse Core Ops, SparseCore 0:
  10.1 46.1 all-gather.1
  64.8 39.8 reduce-scatter.3
  118.0 35.5 reduce-scatter.5
  228.2 12.9 reduce-scatter.7

commit v2 on v0

v2 whole, which is shorter than its diff:
```python
import jax
import jax.numpy as jnp
from jax import lax
from jax.experimental import pallas as pl
from jax.experimental.pallas import tpu as pltpu
from jax.sharding import Mesh
from jax.sharding import PartitionSpec as P

A = 32
B = 16
C = 64
N = 128
SEQ = ("seq_0", "seq_1", "seq_2")
BF = jnp.bfloat16
F32 = jnp.float32
(TOK, FIRST, WROW, GRAD, MIXED, BACK, PRE, GATE, FG_SUM, FG_CH, FG_ALL, ST_X, ST_CH, ST_ALL) = range(14)


def place(s):
    return {"seq_0": s // 16, "seq_1": lax.rem(s // 2, 8), "seq_2": lax.rem(s, 2)}


def nn(x, y):
    return jnp.dot(x, y, preferred_element_type=F32)


def nt(x, y):
    return lax.dot_general(x, y, (((1,), (1,)), ((), ())), preferred_element_type=F32)


def tn(x, y):
    return lax.dot_general(x, y, (((0,), (0,)), ((), ())), preferred_element_type=F32)


def index(shape, dim):
    return lax.broadcasted_iota(jnp.int32, shape, dim)


def one_hot(flags):
    return jnp.where(flags, 1.0, 0.0).astype(BF)


def summed(x, ones):
    high = x.astype(BF)
    low = (x - high.astype(F32)).astype(BF)
    return nn(high, ones) + nn(low, ones)


def kernel(
    tok_ref, cot_ref, first_ref, second_ref, third_ref, w_ref,
    out_ref, ig_ref, gg_ref, fg_ref, st_ref,
    tok_all, tok_t, w_rows, pre_all,
    first_out, first_in, grad_out, grad_in, mixed_out, mixed_in, back_out, back_in,
    second_val, gate_out, gate_in, fg_out, fg_in, fg_ch, fg_fin, st_x, st_ch, st_fin,
    send_sem, recv_sem,
):
    me = lax.axis_index(SEQ)
    ch = lax.axis_index("ch")
    far, half = me // 2, lax.rem(me, 2)
    row, group = me // 4, lax.rem(me, 4)

    def copy(kind, src, dst, where):
        pltpu.make_async_remote_copy(
            src, dst, send_sem.at[kind], recv_sem.at[kind],
            device_id=where, device_id_type=pl.DeviceIdType.MESH,
        ).start()

    def received(kind, part):
        pltpu.make_async_copy(part, part, recv_sem.at[kind]).wait()

    def sent(kind, part):
        pltpu.make_async_copy(part, part, send_sem.at[kind]).wait()

    def to_seq(kind, src, dst):
        def step(d, carry):
            peer = lax.rem(me + d, N)
            copy(kind, src(peer), dst, place(peer))
            return carry

        lax.fori_loop(1, N, step, 0)

    def to_ch(kind, src, dst):
        for d in (1, 2, 3):
            peer = lax.rem(ch + d, 4)
            copy(kind, src(peer), dst, {"ch": peer})

    barrier = pltpu.get_barrier_semaphore()

    def greet(d, carry):
        pl.semaphore_signal(
            barrier, inc=1, device_id=place(lax.rem(me + d, N)), device_id_type=pl.DeviceIdType.MESH
        )
        return carry

    lax.fori_loop(1, N, greet, 0)
    for d in (1, 2, 3):
        pl.semaphore_signal(
            barrier, inc=1, device_id={"ch": lax.rem(ch + d, 4)}, device_id_type=pl.DeviceIdType.MESH
        )

    square = (256, 256)
    r, k = index(square, 0), index(square, 1)
    to_far = one_hot(k == (r & 3) * 64 + (r >> 2))
    to_home = one_hot(k == (r & 63) * 4 + (r >> 6))
    firsts = [first_ref[group * 4 + b] for b in range(4)]
    mixed_first = jnp.concatenate(
        [nn(firsts[b], tok_ref[b * 64 : b * 64 + 64, :]).astype(BF) for b in range(4)], axis=0
    )

    def split_columns(values, buffer):
        ordered = nn(to_far, values).astype(BF)
        for h in range(2):
            buffer[h] = ordered[:, h * 128 : h * 128 + 128].reshape(C, 4, 128)

    def join_columns(buffer):
        return jnp.concatenate([buffer[h].reshape(256, 128) for h in range(2)], axis=1)

    split_columns(mixed_first, first_out)
    first_in[me] = first_out[half, far]
    tok_all[ch] = tok_ref[...]
    w_rows[ch] = w_ref[pl.ds(pl.multiple_of(ch * 256, 256), 256), :]

    own_second, own_third = second_ref[far], third_ref[far]
    rows32 = one_hot((index((512, 32), 0) >> 4) == index((512, 32), 1))
    rows16 = one_hot((index(square[:1] + (16,), 0) & 15) == index(square[:1] + (16,), 1))
    same_a = (r >> 4) == (k >> 4)
    same_b = (index((512, 512), 0) & 15) == (index((512, 512), 1) & 15)

    def spread_third(t):
        return jnp.where(same_b, nt(t.astype(BF), rows32), 0.0).astype(BF)

    def spread_second(t):
        return jnp.where(same_a, nt(t.astype(BF), rows16), 0.0).astype(BF)

    third_mat, third_back = spread_third(nn(rows32, own_third)), spread_third(nt(rows32, own_third))
    second_mat = spread_second(nn(rows16, own_second))
    second_back = spread_second(nt(rows16, own_second))

    pl.semaphore_wait(barrier, N + 2)

    to_ch(TOK, lambda peer: tok_ref, tok_all.at[ch])
    to_seq(FIRST, lambda peer: first_out.at[lax.rem(peer, 2), peer // 2], first_in.at[me])
    to_ch(WROW, lambda peer: w_ref.at[pl.ds(pl.multiple_of(peer * 256, 256), 256), :], w_rows.at[ch])

    received(TOK, tok_all.at[pl.ds(0, 3)])
    gate = nn(tok_all[0], w_ref[0:256, :])
    for p in range(1, 4):
        gate += nn(tok_all[p], w_ref[p * 256 : p * 256 + 256, :])
    sigmoid = jax.nn.sigmoid(gate)
    activation = gate * sigmoid
    upstream = cot_ref[...].astype(F32)
    split_columns((upstream * activation).astype(BF), grad_out)
    grad_in[me] = grad_out[half, far]
    to_seq(GRAD, lambda peer: grad_out.at[lax.rem(peer, 2), peer // 2], grad_in.at[me])
    for p in range(4):
        tok_t[p] = tok_all[p].T

    received(FIRST, first_in.at[pl.ds(0, N - 1)])
    far_first = first_in[...].reshape(512, 128)
    for h in range(2):
        second_val[h * 256 : h * 256 + 256, :] = nn(second_mat, far_first[h * 256 : h * 256 + 256]).astype(BF)
    mixed_out[...] = nn(third_mat, second_val[...]).astype(BF).reshape(N, 4, 128)
    mixed_in[half, far] = mixed_out[me]
    to_seq(MIXED, lambda peer: mixed_out.at[peer], mixed_in.at[half, far])

    received(GRAD, grad_in.at[pl.ds(0, N - 1)])
    far_grad = grad_in[...].reshape(512, 128)
    back_second = nn(third_back, far_grad).astype(BF)
    back_first = jnp.concatenate(
        [nn(second_back, back_second[h * 256 : h * 256 + 256]).astype(BF) for h in range(2)], axis=0
    )
    back_out[...] = back_first.reshape(N, 4, 128)
    back_in[half, far] = back_out[me]
    to_seq(BACK, lambda peer: back_out.at[peer], back_in.at[half, far])

    third_part = jnp.where(same_b, nt(far_grad, second_val[...]), 0.0)
    third_part = summed(jnp.sum(third_part.reshape(A, B, 512), axis=1), rows32)
    second_part = jnp.zeros((16, 256), F32)
    for h in range(2):
        rows = slice(h * 256, h * 256 + 256)
        term = jnp.where(same_a, nt(back_second[rows], far_first[rows]), 0.0)
        second_part += jnp.sum(term.reshape(16, 16, 256), axis=0)
    second_part = summed(second_part, rows16)
    st_x[0] = jnp.concatenate(
        [
            jnp.concatenate([third_part[n * 8 : n * 8 + 8] for n in range(4)], axis=1),
            jnp.concatenate([second_part[0:8], second_part[8:16], jnp.zeros((8, 96), F32)], axis=1),
        ],
        axis=0,
    )
    copy(ST_X, st_x.at[0], st_x.at[1], {"seq_2": 1 - half})

    received(MIXED, first_in.at[pl.ds(0, N - 1)])
    mixed = nn(to_home, join_columns(mixed_in))
    out_ref[...] = (tok_ref[...].astype(F32) + mixed * activation).astype(BF)
    pre_grad = (upstream * mixed * sigmoid * (1.0 + gate * (1.0 - sigmoid))).astype(BF)
    pre_all[ch] = pre_grad
    to_ch(PRE, lambda peer: pre_all.at[ch], pre_all.at[ch])
    for p in range(4):
        gate_out[p * 32 : p * 32 + 32] = nn(tok_t[p], pre_grad).reshape(32, 8, 256).astype(BF)
    gate_in[me] = gate_out[me]
    to_seq(GATE, lambda peer: gate_out.at[peer], gate_in.at[me])

    received(ST_X, st_x.at[1])
    st_ch[ch] = st_x[0] + st_x[1]
    to_ch(ST_CH, lambda peer: st_ch.at[ch], st_ch.at[ch])

    received(BACK, grad_in.at[pl.ds(0, N - 1)])
    back_home = nn(to_home, join_columns(back_in)).astype(BF)
    parts, terms = [], []
    for b in range(4):
        rows = slice(b * 64, b * 64 + 64)
        parts.append(nt(back_home[rows], tok_ref[rows, :]))
        terms.append(tn(firsts[b], back_home[rows]))
    first_part = jnp.concatenate(
        [jnp.concatenate(parts[0:2], axis=0), jnp.concatenate(parts[2:4], axis=0)], axis=1
    )
    fg_out[...] = first_part.reshape(32, 4, 128)
    fg_in[row] = fg_out[row]

    def to_rows(d, carry):
        peer = lax.rem(row + d, 32)
        copy(FG_SUM, fg_out.at[peer], fg_in.at[row], place(peer * 4 + group))
        return carry

    lax.fori_loop(1, 32, to_rows, 0)

    received(ST_CH, st_ch.at[pl.ds(0, 3)])
    st_fin[...] = (st_ch[0] + st_ch[1] + st_ch[2] + st_ch[3]).astype(BF)
    st_ref[far] = st_fin[...]

    def to_columns(d, carry):
        peer = lax.rem(far + d, 64)
        copy(ST_ALL, st_fin, st_ref.at[far], place(peer * 2 + half))
        return carry

    lax.fori_loop(1, 64, to_columns, 0)

    received(PRE, pre_all.at[pl.ds(0, 3)])
    received(WROW, w_rows.at[pl.ds(0, 3)])
    back_gate = nt(pre_all[0], w_rows[0])
    for p in range(1, 4):
        back_gate += nt(pre_all[p], w_rows[p])
    ig_ref[...] = (upstream + jnp.concatenate(terms, axis=0) + back_gate).astype(BF)

    received(FG_SUM, fg_in.at[pl.ds(0, 31)])
    fg_ch[ch] = jnp.sum(fg_in[...], axis=0)
    to_ch(FG_CH, lambda peer: fg_ch.at[ch], fg_ch.at[ch])
    received(FG_CH, fg_ch.at[pl.ds(0, 3)])
    fg_fin[...] = (fg_ch[0] + fg_ch[1] + fg_ch[2] + fg_ch[3]).astype(BF)
    fg_ref[me] = fg_fin[...]
    to_seq(FG_ALL, lambda peer: fg_fin, fg_ref.at[me])

    received(GATE, gate_in.at[pl.ds(0, N - 1)])
    gg_ref[...] = jnp.sum(gate_in[...].astype(F32), axis=0)

    received(ST_ALL, st_ref.at[pl.ds(0, 63)])
    received(FG_ALL, fg_ref.at[pl.ds(0, N - 1)])

    for kind, part in (
        (TOK, tok_all.at[pl.ds(0, 3)]),
        (FIRST, first_in.at[pl.ds(0, N - 1)]),
        (WROW, w_rows.at[pl.ds(0, 3)]),
        (GRAD, grad_in.at[pl.ds(0, N - 1)]),
        (MIXED, first_in.at[pl.ds(0, N - 1)]),
        (BACK, first_in.at[pl.ds(0, N - 1)]),
        (PRE, pre_all.at[pl.ds(0, 3)]),
        (GATE, gate_in.at[pl.ds(0, N - 1)]),
        (FG_SUM, fg_in.at[pl.ds(0, 31)]),
        (FG_CH, fg_ch.at[pl.ds(0, 3)]),
        (FG_ALL, fg_ref.at[pl.ds(0, N - 1)]),
        (ST_X, st_x.at[0]),
        (ST_CH, st_ch.at[pl.ds(0, 3)]),
        (ST_ALL, st_ref.at[pl.ds(0, 63)]),
    ):
        sent(kind, part)


def on_device(tokens, cotangent, first_factor, second_factor, third_factor, gate_weight):
    whole = pl.BlockSpec(memory_space=pltpu.VMEM)
    vm = pltpu.VMEM
    output, input_grad, gate_grad, fg, st = pl.pallas_call(
        kernel,
        out_shape=(
            jax.ShapeDtypeStruct((256, 256), BF),
            jax.ShapeDtypeStruct((256, 256), BF),
            jax.ShapeDtypeStruct((8, 256), F32),
            jax.ShapeDtypeStruct((N, 4, 128), BF),
            jax.ShapeDtypeStruct((C, 16, 128), BF),
        ),
        in_specs=[whole] * 6,
        out_specs=[whole] * 5,
        scratch_shapes=[
            vm((4, 256, 256), BF),
            vm((4, 256, 256), BF),
            vm((4, 256, 256), BF),
            vm((4, 256, 256), BF),
            vm((2, C, 4, 128), BF),
            vm((N, 4, 128), BF),
            vm((2, C, 4, 128), BF),
            vm((N, 4, 128), BF),
            vm((N, 4, 128), BF),
            vm((2, C, 4, 128), BF),
            vm((N, 4, 128), BF),
            vm((2, C, 4, 128), BF),
            vm((512, 128), BF),
            vm((N, 8, 256), BF),
            vm((N, 8, 256), BF),
            vm((32, 4, 128), F32),
            vm((32, 4, 128), F32),
            vm((4, 4, 128), F32),
            vm((4, 128), BF),
            vm((2, 16, 128), F32),
            vm((4, 16, 128), F32),
            vm((16, 128), BF),
            pltpu.SemaphoreType.DMA((14,)),
            pltpu.SemaphoreType.DMA((14,)),
        ],
        compiler_params=pltpu.CompilerParams(
            collective_id=0, has_side_effects=True, vmem_limit_bytes=40 * 1024 * 1024
        ),
    )(tokens, cotangent, first_factor, second_factor, third_factor, gate_weight)
    first_grad = fg.reshape(2, 16, 4, 4, 2, 64).transpose(2, 4, 0, 1, 3, 5).reshape(B, C, C)
    third_grad = st[:, 0:8].reshape(C, 8, 4, 32).transpose(0, 2, 1, 3).reshape(C, A, A)
    second_grad = st[:, 8:16, 0:32].reshape(C, 8, 2, 16).transpose(0, 2, 1, 3).reshape(C, B, B)
    return output, input_grad, first_grad, second_grad, third_grad, gate_grad


def solution(mesh):
    torus = Mesh(mesh.devices.reshape(8, 8, 2, mesh.shape["ch"]), (*SEQ, "ch"))
    return jax.shard_map(
        on_device,
        mesh=torus,
        in_specs=(P(SEQ, "ch"), P(SEQ, "ch"), P(), P(), P(), P(None, "ch")),
        out_specs=(P(SEQ, "ch"), P(SEQ, "ch"), P(), P(), P(), P(SEQ, "ch")),
        check_vma=False,
    )
```

time: 270 us -> 90.1 us (0.33)
  blocking collectives: 128 us -> 0 us
  Pallas kernels: 0 us -> 81.7 us
  waiting for transfers between devices: 54.2 us -> 0 us
  starting transfers between devices: 42.8 us -> 0 us
  between operations: 14.1 us -> 0.75 us
  matrix products: 10.5 us -> 0 us
  local copies, waits for them, and re-layouts: 16.6 us -> 7.49 us
  other arithmetic: 3.4 us -> 0 us
    psum x1 -> x0, blocking collectives: 110 us -> none  [on_device(): lax.psum((first_full, second_full, third_full), SEQ_CH)]
    pallas_call x0 -> x1, Pallas kernels: none -> 81.7 us  [on_device(): pl.pallas_call(kernel, out_shape=(jax.ShapeDtypeStruct((256, 256), BF), j...]
    all_to_all x4 -> x0, starting transfers between devices: 42.7 us -> none  [the longest x1 20.8 us: on_device(): lax.all_to_all(spread(mixed_first), SEQ, split_axis=1, concat_axis=0, til...]
    all_to_all x4 -> x0, waiting for transfers between devices: 32.6 us -> none  [the longest x1 11.8 us: on_device(): lax.all_to_all(spread(mixed_first), SEQ, split_axis=1, concat_axis=0, til...]
    reduce_scatter x3 -> x0, waiting for transfers between devices: 21.5 us -> none  [sum_by_axis(): total = lax.psum_scatter(total, axis, scatter_dimension=0, tiled=True)]
    all_to_all x1 -> x0, blocking collectives: 18.1 us -> none  [on_device(): lax.all_to_all(mixed_far, SEQ, split_axis=0, concat_axis=1, tiled=True)]
    dot_general x12 -> x0, matrix products: 10.5 us -> none  [the longest x1 2.4 us: on_device(): jnp.dot(full_tokens, gate_weight, preferred_element_type=jnp.float32)]
    unnamed x37 -> x13, local copies, waits for them, and re-layouts: 6.28 us -> 4.84 us
  transfers between devices with their start and end apart: 8 -> 0, of which waited for: 4 -> 0; matrix products, arithmetic and copies ran while one was open for 8% -> 0% of each run, Pallas kernels for 0% -> 0%
where the time goes in v2:
time: 90.1 us; the launch traced here: 90 us
  Pallas kernels  81.7 us (91%)
  local copies, waits for them, and re-layouts  7.49 us (8%)
    pallas_call x1, Pallas kernels, on_device(): pl.pallas_call(kernel, out_shape=(jax.ShapeDtypeStruct((256, 256), BF), j...  81.7 us
    unnamed x13, local copies, waits for them, and re-layouts  4.84 us

profile of v2, /device:TPU:1, one launch (start us, length us, event | category | flops | bytes accessed | tf_op | source)
XLA Modules:
  0.0 90.0 jit_solution(215861681877404909)
XLA Ops:
  0.6 0.0 copy-start
  0.6 1.1 %copy.22.second_ref = bf16[64,16,16]{2,1,0:T(8,128)(2,1)S(1)} copy(bf16[64,16,16]{0,2,1:T(8,128)(2,1)} %param.9) | data formatting | bytes 65536 | tf_op args[3]
  1.8 0.0 copy-start.1
  1.8 0.0 copy-start.2
  1.8 0.0 copy-start.3
  1.8 1.8 %copy.23.third_ref = bf16[64,32,32]{2,1,0:T(8,128)(2,1)S(1)} copy(bf16[64,32,32]{0,2,1:T(8,128)(2,1)} %param.10) | data formatting | bytes 262144 | tf_op args[4]
  3.6 0.0 copy-done
  3.6 0.0 copy-done.1
  3.6 0.0 copy-done.2
  3.6 0.0 copy-done.3
  3.6 81.7 %shard_map.109 = (bf16[256,256]{1,0:T(8,128)(2,1)S(1)}, bf16[256,256]{1,0:T(8,128)(2,1)S(1)}, f32[8,256]{1,0:T(8,128)S(1)}, bf16[128,4,128]{2,1,0:T(4,128)(2,1)S(1)}, bf16[64,16,128]{2,1,0:T(8,128)(2,1)S(1)}) custom-call(bf16[256,256]{1,0:T(8,128)(2,1)S(1)} %copy-done.2, bf16[256,256]{1,0:T(8,128)(2,1)S(1)} %copy-done.3, bf16[16,64,64]{2,1,0:T(8,128)(2,1)S(1)} %copy-done.1, ...), custom_call_target="tpu_custom_call" | custom-call | tf_op jit(solution)/shard_map/pallas_call | solution.py:282
  85.4 0.1 copy.25
  85.6 0.6 copy.26
  86.2 0.2 copy.27
  86.4 0.7 copy.28
  87.1 0.1 reshape.30
  87.3 0.8 copy.24
  88.1 0.7 copy.32
  88.7 0.7 copy.33
  89.4 0.6 copy.34
  (2 shorter events, 0.0 us)
Async XLA Ops:
  0.6 3.0 %copy-start = (bf16[1024,256]{1,0:T(8,128)(2,1)S(1)}, bf16[1024,256]{1,0:T(8,128)(2,1)}, u32[]{:S(2)}) copy-start(bf16[1024,256]{1,0:T(8,128)(2,1)} %w_ref.1) | copy-start | bytes 1572868
  1.8 1.8 %copy-start.1 = (bf16[16,64,64]{2,1,0:T(8,128)(2,1)S(1)}, bf16[16,64,64]{2,1,0:T(8,128)(2,1)}, u32[]{:S(2)}) copy-start(bf16[16,64,64]{2,1,0:T(8,128)(2,1)} %first_ref.1) | copy-start | bytes 393220
  1.8 1.8 %copy-start.2 = (bf16[256,256]{1,0:T(8,128)(2,1)S(1)}, bf16[256,256]{1,0:T(8,128)(2,1)}, u32[]{:S(2)}) copy-start(bf16[256,256]{1,0:T(8,128)(2,1)} %tok_ref.1) | copy-start | bytes 393220
  1.8 1.8 %copy-start.3 = (bf16[256,256]{1,0:T(8,128)(2,1)S(1)}, bf16[256,256]{1,0:T(8,128)(2,1)}, u32[]{:S(2)}) copy-start(bf16[256,256]{1,0:T(8,128)(2,1)} %cot_ref.1) | copy-start | bytes 393220

commit v3 on v2

v3 whole, which is shorter than its diff:
```python
import jax
import jax.numpy as jnp
from jax import lax
from jax.experimental import pallas as pl
from jax.experimental.pallas import tpu as pltpu
from jax.sharding import Mesh
from jax.sharding import PartitionSpec as P

A = 32
B = 16
C = 64
N = 128
SEQ = ("seq_0", "seq_1", "seq_2")
BF = jnp.bfloat16
F32 = jnp.float32
(
    TOK, TOK_FAR, TOK_LAST, FIRST, WROW, GRAD, MIXED, BACK, PRE, PRE_FAR, PRE_LAST,
    GATE_A, GATE_B, GATE_A2, GATE_B2, GATE_X, FG_SUM, FG_CH, FG_ALL, ST_X, ST_CH, ST_ALL,
) = range(22)


def place(s):
    return {"seq_0": s // 16, "seq_1": lax.rem(s // 2, 8), "seq_2": lax.rem(s, 2)}


def nn(x, y):
    return jnp.dot(x, y, preferred_element_type=F32)


def nt(x, y):
    return lax.dot_general(x, y, (((1,), (1,)), ((), ())), preferred_element_type=F32)


def tn(x, y):
    return lax.dot_general(x, y, (((0,), (0,)), ((), ())), preferred_element_type=F32)


def index(shape, dim):
    return lax.broadcasted_iota(jnp.int32, shape, dim)


def one_hot(flags):
    return jnp.where(flags, 1.0, 0.0).astype(BF)


def summed(x, ones):
    high = x.astype(BF)
    low = (x - high.astype(F32)).astype(BF)
    return nn(high, ones) + nn(low, ones)


def kernel(
    tok_hbm, cot_hbm, first_hbm, second_hbm, third_hbm, w_hbm,
    out_ref, ig_ref, gg_ref, fg_ref, st_ref,
    tok_ref, cot_ref, first_ref, second_ref, third_ref, w_ref,
    tok_all, tok_t, w_rows, pre_all,
    first_out, first_in, grad_out, grad_in, mixed_out, mixed_in, back_out, back_in,
    second_val, gate_a, gate_a_in, gate_b, gate_b_in, gate_a2, gate_a2_in, gate_b2, gate_b2_in,
    gate_x, gate_x_in, fg_out, fg_in, fg_ch, fg_fin, st_x, st_ch, st_fin,
    send_sem, recv_sem, load_sem, y_sem, x_sem,
):
    me = lax.axis_index(SEQ)
    ch = lax.axis_index("ch")
    far, half = me // 2, lax.rem(me, 2)
    row, group = me // 4, lax.rem(me, 4)
    at_z, at_y = me // 16, lax.rem(me // 2, 8)
    chip, core = ch // 2, lax.rem(ch, 2)
    sibling = chip * 2 + 1 - core
    across = (1 - chip) * 2 + core

    def copy(kind, src, dst, where):
        pltpu.make_async_remote_copy(
            src, dst, send_sem.at[kind], recv_sem.at[kind],
            device_id=where, device_id_type=pl.DeviceIdType.MESH,
        ).start()

    def greet(sem, where):
        pl.semaphore_signal(sem, inc=1, device_id=where, device_id_type=pl.DeviceIdType.MESH)

    def received(kind, part):
        pltpu.make_async_copy(part, part, recv_sem.at[kind]).wait()

    def sent(kind, part):
        pltpu.make_async_copy(part, part, send_sem.at[kind]).wait()

    def to_seq(kind, src, dst, first=1, last=N):
        def step(d, carry):
            peer = lax.rem(me + d, N)
            copy(kind, src(peer), dst, place(peer))
            return carry

        lax.fori_loop(first, last, step, 0)

    def to_ch(kind, src, dst):
        for d in (1, 2, 3):
            peer = lax.rem(ch + d, 4)
            copy(kind, src(peer), dst, {"ch": peer})

    def share(kind, buffer):
        copy(kind + 1, buffer.at[ch], buffer.at[ch], {"ch": across})
        copy(kind, buffer.at[ch], buffer.at[ch], {"ch": sibling})

    def pass_on(kind, buffer):
        received(kind + 1, buffer.at[across])
        copy(kind + 2, buffer.at[across], buffer.at[across], {"ch": sibling})

    barrier = pltpu.get_barrier_semaphore()
    for d in range(1, 8):
        greet(barrier, {"seq_0": lax.rem(at_z + d, 8)})
        greet(barrier, {"seq_1": lax.rem(at_y + d, 8)})
    greet(barrier, {"seq_2": 1 - half})
    for d in (1, 2, 3):
        greet(barrier, {"ch": lax.rem(ch + d, 4)})
    loads = [
        pltpu.make_async_copy(src, dst, load_sem.at[n])
        for n, (src, dst) in enumerate(
            (
                (tok_hbm, tok_ref), (first_hbm, first_ref), (second_hbm, second_ref),
                (third_hbm, third_ref), (cot_hbm, cot_ref), (w_hbm, w_ref),
            )
        )
    ]
    for load in loads:
        load.start()

    square = (256, 256)
    r, k = index(square, 0), index(square, 1)
    to_far = one_hot(k == (r & 3) * 64 + (r >> 2))
    to_home = one_hot(k == (r & 63) * 4 + (r >> 6))
    loads[0].wait()
    tok_all[ch] = nn(to_far, tok_ref[...]).astype(BF)
    loads[1].wait()
    spread_d = one_hot((index((64, 256), 1) & 63) == index((64, 256), 0))
    first_big = nn(jnp.concatenate([first_ref[group * 4 + b] for b in range(4)], axis=0), spread_d)
    first_big = jnp.where((r >> 6) == (k >> 6), first_big, 0.0).astype(BF)
    first_mat = nn(nn(to_far, first_big).astype(BF), to_home).astype(BF)
    first_back = nn(nt(to_far, first_big).astype(BF), to_home).astype(BF)

    def split_columns(values, buffer):
        for h in range(2):
            buffer[h] = values[:, h * 128 : h * 128 + 128].reshape(C, 4, 128)

    def join_columns(buffer):
        return jnp.concatenate([buffer[h].reshape(256, 128) for h in range(2)], axis=1)

    split_columns(nn(first_mat, tok_all[ch]).astype(BF), first_out)
    first_in[me] = first_out[half, far]

    rows32 = one_hot((index((512, 32), 0) >> 4) == index((512, 32), 1))
    rows16 = one_hot((index((256, 16), 0) & 15) == index((256, 16), 1))
    same_a = (r >> 4) == (k >> 4)
    same_b = (index((512, 512), 0) & 15) == (index((512, 512), 1) & 15)

    def own(ref, size):
        shape = (size, size, C)
        return jnp.sum(jnp.where(index(shape, 2) == far, ref[...].astype(F32), 0.0), axis=2).astype(BF)

    def spread_third(t):
        return jnp.where(same_b, nt(t.astype(BF), rows32), 0.0).astype(BF)

    def spread_second(t):
        return jnp.where(same_a, nt(t.astype(BF), rows16), 0.0).astype(BF)

    loads[2].wait()
    own_second = own(second_ref, B)
    second_mat = spread_second(nn(rows16, own_second))
    second_back = spread_second(nt(rows16, own_second))
    loads[3].wait()
    own_third = own(third_ref, A)
    third_mat, third_back = spread_third(nn(rows32, own_third)), spread_third(nt(rows32, own_third))
    loads[4].wait()
    upstream = nn(to_far, cot_ref[...])
    loads[5].wait()
    w_rows[ch] = w_ref[pl.ds(pl.multiple_of(ch * 256, 256), 256), :]

    def gate_term(p):
        return nn(tok_all[p], w_ref[pl.ds(pl.multiple_of(p * 256, 256), 256), :])

    gate = gate_term(ch)

    pl.semaphore_wait(barrier, 18)

    share(TOK, tok_all)
    for d in range(1, 8):
        greet(y_sem, {"seq_1": lax.rem(at_y + d, 8)})
    pl.semaphore_wait(y_sem, 7)
    greet(x_sem, {"seq_2": 1 - half})
    pl.semaphore_wait(x_sem, 1)

    def first_for(peer):
        return first_out.at[lax.rem(peer, 2), peer // 2]

    to_seq(FIRST, first_for, first_in.at[me], 1, 64)
    pass_on(TOK, tok_all)
    to_seq(FIRST, first_for, first_in.at[me], 64, N)

    received(TOK, tok_all.at[sibling])
    gate += gate_term(sibling) + gate_term(across)
    received(TOK_LAST, tok_all.at[0])
    gate += gate_term((1 - chip) * 2 + 1 - core)
    sigmoid = jax.nn.sigmoid(gate)
    activation = gate * sigmoid
    split_columns((upstream * activation).astype(BF), grad_out)
    grad_in[me] = grad_out[half, far]
    to_seq(GRAD, lambda peer: grad_out.at[lax.rem(peer, 2), peer // 2], grad_in.at[me])

    received(FIRST, first_in.at[pl.ds(0, N - 1)])
    far_first = first_in[...].reshape(512, 128)
    for h in range(2):
        second_val[h * 256 : h * 256 + 256, :] = nn(second_mat, far_first[h * 256 : h * 256 + 256]).astype(BF)
    mixed_out[...] = nn(third_mat, second_val[...]).astype(BF).reshape(N, 4, 128)
    mixed_in[half, far] = mixed_out[me]
    to_seq(MIXED, lambda peer: mixed_out.at[peer], mixed_in.at[half, far])
    to_ch(WROW, lambda peer: w_ref.at[pl.ds(pl.multiple_of(peer * 256, 256), 256), :], w_rows.at[ch])
    for p in range(4):
        tok_t[p] = tok_all[p].T

    received(GRAD, grad_in.at[pl.ds(0, N - 1)])
    far_grad = grad_in[...].reshape(512, 128)
    back_second = nn(third_back, far_grad).astype(BF)
    back_first = jnp.concatenate(
        [nn(second_back, back_second[h * 256 : h * 256 + 256]).astype(BF) for h in range(2)], axis=0
    )
    back_out[...] = back_first.reshape(N, 4, 128)
    back_in[half, far] = back_out[me]
    to_seq(BACK, lambda peer: back_out.at[peer], back_in.at[half, far])

    received(MIXED, first_in.at[pl.ds(0, N - 1)])
    mixed = join_columns(mixed_in).astype(F32)
    pre_grad = (upstream * mixed * sigmoid * (1.0 + gate * (1.0 - sigmoid))).astype(BF)
    pre_all[ch] = pre_grad
    share(PRE, pre_all)
    for p in range(4):
        term = nn(tok_t[p], pre_grad)
        gate_a[2 * p : 2 * p + 2] = term[:, 0:128].reshape(2, 128, 128).astype(BF)
        for n in range(16):
            gate_b[n % 8, 2 * p + n // 8] = term[n * 16 : n * 16 + 16, 128:256].astype(BF)
    gate_a_in[at_z] = gate_a[at_z]
    gate_b_in[at_y] = gate_b[at_y]
    for d in range(1, 8):
        peer_z, peer_y = lax.rem(at_z + d, 8), lax.rem(at_y + d, 8)
        copy(GATE_A, gate_a.at[peer_z], gate_a_in.at[at_z], {"seq_0": peer_z})
        copy(GATE_B, gate_b.at[peer_y], gate_b_in.at[at_y], {"seq_1": peer_y})

    third_part = jnp.where(same_b, nt(far_grad, second_val[...]), 0.0)
    third_part = summed(jnp.sum(third_part.reshape(A, B, 512), axis=1), rows32)
    second_part = jnp.zeros((16, 256), F32)
    for h in range(2):
        rows = slice(h * 256, h * 256 + 256)
        term = jnp.where(same_a, nt(back_second[rows], far_first[rows]), 0.0)
        second_part += jnp.sum(term.reshape(16, 16, 256), axis=0)
    second_part = summed(second_part, rows16)
    st_x[0] = jnp.concatenate(
        [
            jnp.concatenate([third_part[n * 8 : n * 8 + 8] for n in range(4)], axis=1),
            jnp.concatenate([second_part[0:8], second_part[8:16], jnp.zeros((8, 96), F32)], axis=1),
        ],
        axis=0,
    )
    copy(ST_X, st_x.at[0], st_x.at[1], {"seq_2": 1 - half})
    pass_on(PRE, pre_all)

    received(BACK, grad_in.at[pl.ds(0, N - 1)])
    back_home = join_columns(back_in)
    first_part = jnp.where((r & 3) == (k & 3), nt(back_home, tok_all[ch]), 0.0)
    first_part = summed(first_part, one_hot((index((256, 64), 0) >> 2) == index((256, 64), 1)))
    fg_out[...] = jnp.concatenate([first_part[0:128], first_part[128:256]], axis=1).reshape(32, 4, 128)
    fg_in[row] = fg_out[row]

    def to_rows(d, carry):
        peer = lax.rem(row + d, 32)
        copy(FG_SUM, fg_out.at[peer], fg_in.at[row], place(peer * 4 + group))
        return carry

    lax.fori_loop(1, 32, to_rows, 0)

    received(ST_X, st_x.at[1])
    st_ch[ch] = st_x[0] + st_x[1]
    to_ch(ST_CH, lambda peer: st_ch.at[ch], st_ch.at[ch])

    received(GATE_A, gate_a_in.at[pl.ds(0, 7)])
    gate_a2[...] = jnp.sum(gate_a_in[...].astype(F32), axis=0).astype(BF).reshape(8, 16, 128)
    received(GATE_B, gate_b_in.at[pl.ds(0, 7)])
    gate_b2[...] = jnp.sum(gate_b_in[...].astype(F32), axis=0).astype(BF)
    gate_a2_in[at_y] = gate_a2[at_y]
    gate_b2_in[at_z] = gate_b2[at_z]
    for d in range(1, 8):
        peer_z, peer_y = lax.rem(at_z + d, 8), lax.rem(at_y + d, 8)
        copy(GATE_A2, gate_a2.at[peer_y], gate_a2_in.at[at_y], {"seq_1": peer_y})
        copy(GATE_B2, gate_b2.at[peer_z], gate_b2_in.at[at_z], {"seq_0": peer_z})

    received(FG_SUM, fg_in.at[pl.ds(0, 31)])
    fg_ch[ch] = jnp.sum(fg_in[...], axis=0)
    to_ch(FG_CH, lambda peer: fg_ch.at[ch], fg_ch.at[ch])

    received(ST_CH, st_ch.at[pl.ds(0, 3)])
    st_fin[...] = (st_ch[0] + st_ch[1] + st_ch[2] + st_ch[3]).astype(BF)
    st_ref[far] = st_fin[...]

    def to_columns(d, carry):
        peer = lax.rem(far + d, 64)
        copy(ST_ALL, st_fin, st_ref.at[far], place(peer * 2 + half))
        return carry

    lax.fori_loop(1, 64, to_columns, 0)

    received(FG_CH, fg_ch.at[pl.ds(0, 3)])
    fg_fin[...] = (fg_ch[0] + fg_ch[1] + fg_ch[2] + fg_ch[3]).astype(BF)
    fg_ref[me] = fg_fin[...]
    to_seq(FG_ALL, lambda peer: fg_fin, fg_ref.at[me])

    received(GATE_A2, gate_a2_in.at[pl.ds(0, 7)])
    received(GATE_B2, gate_b2_in.at[pl.ds(0, 7)])
    gate_sum = jnp.concatenate(
        [jnp.sum(part[...].astype(F32), axis=0) for part in (gate_a2_in, gate_b2_in)], axis=1
    )
    gate_x[0] = gate_sum[0:8]
    gate_x[1] = gate_sum[8:16]
    copy(GATE_X, gate_x.at[1 - half], gate_x_in, {"seq_2": 1 - half})

    out_ref[...] = nn(to_home, (tok_all[ch].astype(F32) + mixed * activation).astype(BF)).astype(BF)
    received(PRE, pre_all.at[0])
    received(PRE_LAST, pre_all.at[0])
    received(WROW, w_rows.at[pl.ds(0, 3)])
    in_grad = upstream + nn(first_back, back_home)
    for p in range(4):
        in_grad += nt(pre_all[p], w_rows[p])
    ig_ref[...] = nn(to_home, in_grad.astype(BF)).astype(BF)
    received(GATE_X, gate_x_in)
    gg_ref[...] = gate_x[half] + gate_x_in[...]

    received(ST_ALL, st_ref.at[pl.ds(0, 63)])
    received(FG_ALL, fg_ref.at[pl.ds(0, N - 1)])

    for kind, part in (
        (TOK, tok_all.at[0]),
        (TOK_FAR, tok_all.at[0]),
        (TOK_LAST, tok_all.at[0]),
        (FIRST, first_in.at[pl.ds(0, N - 1)]),
        (WROW, w_rows.at[pl.ds(0, 3)]),
        (GRAD, grad_in.at[pl.ds(0, N - 1)]),
        (MIXED, first_in.at[pl.ds(0, N - 1)]),
        (BACK, first_in.at[pl.ds(0, N - 1)]),
        (PRE, pre_all.at[0]),
        (PRE_FAR, pre_all.at[0]),
        (PRE_LAST, pre_all.at[0]),
        (GATE_A, gate_a_in.at[pl.ds(0, 7)]),
        (GATE_B, gate_b_in.at[pl.ds(0, 7)]),
        (GATE_A2, gate_a2_in.at[pl.ds(0, 7)]),
        (GATE_B2, gate_b2_in.at[pl.ds(0, 7)]),
        (GATE_X, gate_x_in),
        (FG_SUM, fg_in.at[pl.ds(0, 31)]),
        (FG_CH, fg_ch.at[pl.ds(0, 3)]),
        (FG_ALL, fg_ref.at[pl.ds(0, N - 1)]),
        (ST_X, st_x.at[0]),
        (ST_CH, st_ch.at[pl.ds(0, 3)]),
        (ST_ALL, st_ref.at[pl.ds(0, 63)]),
    ):
        sent(kind, part)


def on_device(tokens, cotangent, first_factor, second_factor, third_factor, gate_weight):
    whole = pl.BlockSpec(memory_space=pltpu.VMEM)
    vm = pltpu.VMEM
    output, input_grad, gate_grad, fg, st = pl.pallas_call(
        kernel,
        out_shape=(
            jax.ShapeDtypeStruct((256, 256), BF),
            jax.ShapeDtypeStruct((256, 256), BF),
            jax.ShapeDtypeStruct((8, 256), F32),
            jax.ShapeDtypeStruct((N, 4, 128), BF),
            jax.ShapeDtypeStruct((C, 16, 128), BF),
        ),
        in_specs=[pl.BlockSpec(memory_space=pl.ANY)] * 6,
        out_specs=[whole] * 5,
        scratch_shapes=[
            vm((256, 256), BF),
            vm((256, 256), BF),
            vm((B, C, C), BF),
            vm((B, B, C), BF),
            vm((A, A, C), BF),
            vm((1024, 256), BF),
            *[vm((4, 256, 256), BF)] * 4,
            vm((2, C, 4, 128), BF),
            vm((N, 4, 128), BF),
            vm((2, C, 4, 128), BF),
            vm((N, 4, 128), BF),
            vm((N, 4, 128), BF),
            vm((2, C, 4, 128), BF),
            vm((N, 4, 128), BF),
            vm((2, C, 4, 128), BF),
            vm((512, 128), BF),
            *[vm((8, 128, 128), BF)] * 2,
            *[vm((8, 8, 16, 128), BF)] * 2,
            *[vm((8, 16, 128), BF)] * 4,
            vm((2, 8, 256), F32),
            vm((8, 256), F32),
            vm((32, 4, 128), F32),
            vm((32, 4, 128), F32),
            vm((4, 4, 128), F32),
            vm((4, 128), BF),
            vm((2, 16, 128), F32),
            vm((4, 16, 128), F32),
            vm((16, 128), BF),
            pltpu.SemaphoreType.DMA((22,)),
            pltpu.SemaphoreType.DMA((22,)),
            pltpu.SemaphoreType.DMA((6,)),
            pltpu.SemaphoreType.REGULAR,
            pltpu.SemaphoreType.REGULAR,
        ],
        compiler_params=pltpu.CompilerParams(
            collective_id=0, has_side_effects=True, vmem_limit_bytes=56 * 1024 * 1024
        ),
    )(
        tokens,
        cotangent,
        first_factor,
        second_factor.transpose(1, 2, 0),
        third_factor.transpose(1, 2, 0),
        gate_weight,
    )
    first_grad = fg.reshape(32, 4, 4, 2, 64).transpose(1, 2, 3, 0, 4).reshape(B, C, C)
    third_grad = st[:, 0:8].reshape(C, 8, 4, 32).transpose(0, 2, 1, 3).reshape(C, A, A)
    second_grad = st[:, 8:16, 0:32].reshape(C, 8, 2, 16).transpose(0, 2, 1, 3).reshape(C, B, B)
    return output, input_grad, first_grad, second_grad, third_grad, gate_grad


def solution(mesh):
    torus = Mesh(mesh.devices.reshape(8, 8, 2, mesh.shape["ch"]), (*SEQ, "ch"))
    return jax.shard_map(
        on_device,
        mesh=torus,
        in_specs=(P(SEQ, "ch"), P(SEQ, "ch"), P(), P(), P(), P(None, "ch")),
        out_specs=(P(SEQ, "ch"), P(SEQ, "ch"), P(), P(), P(), P(SEQ, "ch")),
        check_vma=False,
    )
```

time: 90.1 us -> 73.1 us (0.81)
  Pallas kernels: 81.7 us -> 66 us
  local copies, waits for them, and re-layouts: 7.49 us -> 6.21 us
    pallas_call x1, Pallas kernels: 81.7 us -> 66 us  [on_device(): pl.pallas_call(kernel, out_shape=(jax.ShapeDtypeStruct((256, 256), BF), j...]
    unnamed x13, local copies, waits for them, and re-layouts: 4.84 us -> 2.59 us
    slice x2, local copies, waits for them, and re-layouts: 0.21 us -> 1.17 us  [on_device(): st[:, 0:8].reshape(C, 8, 4, 32).transpose(0, 2, 1, 3).reshape(C, A, A)]
where the time goes in v3:
time: 73.1 us; the launch traced here: 72.9 us
  Pallas kernels  66 us (90%)
  local copies, waits for them, and re-layouts  6.21 us (8%)
    pallas_call x1, Pallas kernels, on_device(): pl.pallas_call(kernel, out_shape=(jax.ShapeDtypeStruct((256, 256), BF), j...  66 us
    unnamed x13, local copies, waits for them, and re-layouts  2.59 us

profile of v3, /device:TPU:1, one launch (start us, length us, event | category | flops | bytes accessed | tf_op | source)
XLA Modules:
  0.0 72.9 jit_solution(14113205824078031684)
XLA Ops:
  0.6 66.0 %shard_map.109 = (bf16[256,256]{1,0:T(8,128)(2,1)}, bf16[256,256]{1,0:T(8,128)(2,1)}, f32[8,256]{1,0:T(8,128)}, bf16[128,4,128]{2,1,0:T(4,128)(2,1)}, bf16[64,16,128]{2,1,0:T(8,128)(2,1)}) custom-call(bf16[256,256]{1,0:T(8,128)(2,1)} %tok_hbm.1, bf16[256,256]{1,0:T(8,128)(2,1)} %cot_hbm.1, bf16[16,64,64]{2,1,0:T(8,128)(2,1)} %first_hbm.1, ...), custom_call_target="tpu_custom_call" | custom-call | tf_op jit(solution)/shard_map/pallas_call | solution.py:365
  66.6 0.0 copy-start
  66.6 1.0 %slice.7 = bf16[64,8,128]{2,1,0:T(8,128)(2,1)S(1)} slice(bf16[64,16,128]{2,1,0:T(8,128)(2,1)} %get-tuple-element.14), slice={[0:64], [0:8], [0:128]} | slice | bytes 262144 | tf_op jit(solution)/shard_map/slice | solution.py:423
  67.6 0.0 copy-done
  67.6 0.1 copy.19
  67.8 0.6 copy.20
  68.4 0.2 copy.21
  68.6 0.0 copy-start.1
  68.6 0.7 copy.22
  69.4 0.2 copy-done.1
  69.6 0.1 reshape.30
  69.7 0.0 copy-start.3
  69.7 0.8 %copy.18 = bf16[4,4,2,32,64]{4,3,2,1,0:T(8,128)(2,1)} copy(bf16[4,4,2,32,64]{4,2,1,0,3:T(2,128)(2,1)S(1)} %bitcast.13) | data formatting | bytes 262144 | tf_op jit(solution)/shard_map/transpose | solution.py:422
  70.5 0.1 copy-done.3
  70.6 0.0 copy-start.2
  70.6 0.7 copy.26
  71.3 0.3 copy-done.2
  71.6 0.0 copy-start.4
  71.6 0.7 copy.27
  72.2 0.0 copy-done.4
  72.3 0.6 copy.28
  (1 shorter events, 0.0 us)
Async XLA Ops:
  66.6 1.0 %copy-start = (bf16[64,16,128]{2,1,0:T(8,128)(2,1)S(1)}, bf16[64,16,128]{2,1,0:T(8,128)(2,1)}, u32[]{:S(2)}) copy-start(bf16[64,16,128]{2,1,0:T(8,128)(2,1)} %get-tuple-element.14) | copy-start | bytes 786436
  68.6 1.0 %copy-start.1 = (bf16[128,4,128]{2,1,0:T(4,128)(2,1)S(1)}, bf16[128,4,128]{2,1,0:T(4,128)(2,1)}, u32[]{:S(2)}) copy-start(bf16[128,4,128]{2,1,0:T(4,128)(2,1)} %get-tuple-element.13) | copy-start | bytes 393220
  69.7 0.9 %copy-start.3 = (bf16[256,256]{1,0:T(8,128)(2,1)S(1)}, bf16[256,256]{1,0:T(8,128)(2,1)}, u32[]{:S(2)}) copy-start(bf16[256,256]{1,0:T(8,128)(2,1)} %get-tuple-element.22) | copy-start | bytes 393220
  70.6 1.0 %copy-start.2 = (bf16[256,256]{1,0:T(8,128)(2,1)S(1)}, bf16[256,256]{1,0:T(8,128)(2,1)}, u32[]{:S(2)}) copy-start(bf16[256,256]{1,0:T(8,128)(2,1)} %get-tuple-element.23) | copy-start | bytes 393220
  71.6 0.7 copy-start.4

commit v4 on v3

--- a/solution.py
+++ b/solution.py
@@ -14,9 +14,9 @@
 BF = jnp.bfloat16
 F32 = jnp.float32
 (
-    TOK, TOK_FAR, TOK_LAST, FIRST, WROW, GRAD, MIXED, BACK, PRE, PRE_FAR, PRE_LAST,
+    TOK, TOK_FAR, TOK_LAST, FIRST, GRAD, MIXED, BACK, PAIR, ACROSS,
     GATE_A, GATE_B, GATE_A2, GATE_B2, GATE_X, FG_SUM, FG_CH, FG_ALL, ST_X, ST_CH, ST_ALL,
-) = range(22)
+) = range(20)
 
 
 def place(s):
@@ -51,13 +51,14 @@
 
 def kernel(
     tok_hbm, cot_hbm, first_hbm, second_hbm, third_hbm, w_hbm,
-    out_ref, ig_ref, gg_ref, fg_ref, st_ref,
+    out_hbm, ig_hbm, gg_hbm, first_hbm_grad, second_hbm_grad, third_hbm_grad,
+    out_ref, ig_ref, gg_ref, first_grad, second_grad, third_grad,
     tok_ref, cot_ref, first_ref, second_ref, third_ref, w_ref,
-    tok_all, tok_t, w_rows, pre_all,
+    tok_all, tok_t, pair_out, pair_in, across_out, across_in, input_part,
     first_out, first_in, grad_out, grad_in, mixed_out, mixed_in, back_out, back_in,
     second_val, gate_a, gate_a_in, gate_b, gate_b_in, gate_a2, gate_a2_in, gate_b2, gate_b2_in,
-    gate_x, gate_x_in, fg_out, fg_in, fg_ch, fg_fin, st_x, st_ch, st_fin,
-    send_sem, recv_sem, load_sem, y_sem, x_sem,
+    gate_x, gate_x_in, fg_out, fg_in, fg_ch, fg_fin, fg_ref, st_x, st_ch, st_fin, st_ref, st_rows,
+    send_sem, recv_sem, load_sem, store_sem, y_sem, x_sem,
 ):
     me = lax.axis_index(SEQ)
     ch = lax.axis_index("ch")
@@ -67,6 +68,7 @@
     chip, core = ch // 2, lax.rem(ch, 2)
     sibling = chip * 2 + 1 - core
     across = (1 - chip) * 2 + core
+    corner = (1 - chip) * 2 + 1 - core
 
     def copy(kind, src, dst, where):
         pltpu.make_async_remote_copy(
@@ -122,6 +124,15 @@
     ]
     for load in loads:
         load.start()
+    stores = [
+        pltpu.make_async_copy(src, dst, store_sem.at[n])
+        for n, (src, dst) in enumerate(
+            (
+                (out_ref, out_hbm), (ig_ref, ig_hbm), (gg_ref, gg_hbm),
+                (first_grad, first_hbm_grad), (second_grad, second_hbm_grad), (third_grad, third_hbm_grad),
+            )
+        )
+    ]
 
     square = (256, 256)
     r, k = index(square, 0), index(square, 1)
@@ -171,10 +182,12 @@
     loads[4].wait()
     upstream = nn(to_far, cot_ref[...])
     loads[5].wait()
-    w_rows[ch] = w_ref[pl.ds(pl.multiple_of(ch * 256, 256), 256), :]
+
+    def w_rows(p):
+        return w_ref[pl.ds(pl.multiple_of(p * 256, 256), 256), :]
 
     def gate_term(p):
-        return nn(tok_all[p], w_ref[pl.ds(pl.multiple_of(p * 256, 256), 256), :])
+        return nn(tok_all[p], w_rows(p))
 
     gate = gate_term(ch)
 
@@ -197,7 +210,7 @@
     received(TOK, tok_all.at[sibling])
     gate += gate_term(sibling) + gate_term(across)
     received(TOK_LAST, tok_all.at[0])
-    gate += gate_term((1 - chip) * 2 + 1 - core)
+    gate += gate_term(corner)
     sigmoid = jax.nn.sigmoid(gate)
     activation = gate * sigmoid
     split_columns((upstream * activation).astype(BF), grad_out)
@@ -211,7 +224,6 @@
     mixed_out[...] = nn(third_mat, second_val[...]).astype(BF).reshape(N, 4, 128)
     mixed_in[half, far] = mixed_out[me]
     to_seq(MIXED, lambda peer: mixed_out.at[peer], mixed_in.at[half, far])
-    to_ch(WROW, lambda peer: w_ref.at[pl.ds(pl.multiple_of(peer * 256, 256), 256), :], w_rows.at[ch])
     for p in range(4):
         tok_t[p] = tok_all[p].T
 
@@ -228,8 +240,6 @@
     received(MIXED, first_in.at[pl.ds(0, N - 1)])
     mixed = join_columns(mixed_in).astype(F32)
     pre_grad = (upstream * mixed * sigmoid * (1.0 + gate * (1.0 - sigmoid))).astype(BF)
-    pre_all[ch] = pre_grad
-    share(PRE, pre_all)
     for p in range(4):
         term = nn(tok_t[p], pre_grad)
         gate_a[2 * p : 2 * p + 2] = term[:, 0:128].reshape(2, 128, 128).astype(BF)
@@ -241,6 +251,12 @@
         peer_z, peer_y = lax.rem(at_z + d, 8), lax.rem(at_y + d, 8)
         copy(GATE_A, gate_a.at[peer_z], gate_a_in.at[at_z], {"seq_0": peer_z})
         copy(GATE_B, gate_b.at[peer_y], gate_b_in.at[at_y], {"seq_1": peer_y})
+
+    pair_out[0] = nt(pre_grad, w_rows(sibling)).astype(BF)
+    pair_out[1] = nt(pre_grad, w_rows(corner)).astype(BF)
+    copy(PAIR, pair_out, pair_in, {"ch": sibling})
+    input_part[0] = nt(pre_grad, w_rows(ch))
+    input_part[1] = nt(pre_grad, w_rows(across))
 
     third_part = jnp.where(same_b, nt(far_grad, second_val[...]), 0.0)
     third_part = summed(jnp.sum(third_part.reshape(A, B, 512), axis=1), rows32)
@@ -258,7 +274,9 @@
         axis=0,
     )
     copy(ST_X, st_x.at[0], st_x.at[1], {"seq_2": 1 - half})
-    pass_on(PRE, pre_all)
+    received(PAIR, pair_in)
+    across_out[...] = (input_part[1] + pair_in[1].astype(F32)).astype(BF)
+    copy(ACROSS, across_out, across_in, {"ch": across})
 
     received(BACK, grad_in.at[pl.ds(0, N - 1)])
     back_home = join_columns(back_in)
@@ -319,31 +337,51 @@
     copy(GATE_X, gate_x.at[1 - half], gate_x_in, {"seq_2": 1 - half})
 
     out_ref[...] = nn(to_home, (tok_all[ch].astype(F32) + mixed * activation).astype(BF)).astype(BF)
-    received(PRE, pre_all.at[0])
-    received(PRE_LAST, pre_all.at[0])
-    received(WROW, w_rows.at[pl.ds(0, 3)])
-    in_grad = upstream + nn(first_back, back_home)
-    for p in range(4):
-        in_grad += nt(pre_all[p], w_rows[p])
+    stores[0].start()
+    received(ACROSS, across_in)
+    in_grad = upstream + nn(first_back, back_home) + input_part[0]
+    in_grad += pair_in[0].astype(F32) + across_in[...].astype(F32)
     ig_ref[...] = nn(to_home, in_grad.astype(BF)).astype(BF)
+    stores[1].start()
     received(GATE_X, gate_x_in)
     gg_ref[...] = gate_x[half] + gate_x_in[...]
-
+    stores[2].start()
+
+    by_part = one_hot(k == (r & 15) * 16 + (r >> 4))
+    by_block = one_hot(
+        index((512, 512), 1) == (index((512, 512), 0) & 31) * 16 + (index((512, 512), 0) >> 5)
+    )
+    eye = one_hot(index((128, 128), 0) == index((128, 128), 1))
     received(ST_ALL, st_ref.at[pl.ds(0, 63)])
+    for g in range(4):
+        block = st_ref[g * 16 : g * 16 + 16].reshape(256, 128)
+        st_rows[:, g * 16 : g * 16 + 16, :] = nn(by_part, block).astype(BF).reshape(16, 16, 128)
+    for n in range(8):
+        turned = nt(eye, st_rows[n]).astype(BF)
+        for m in range(4):
+            third_grad[m * 8 + n] = turned[m * 32 : m * 32 + 32]
+    stores[5].start()
+    for n in range(8):
+        turned = nt(eye[0:32], st_rows[8 + n]).astype(BF)
+        for m in range(2):
+            second_grad[m * 8 + n] = turned[m * 16 : m * 16 + 16]
+    stores[4].start()
     received(FG_ALL, fg_ref.at[pl.ds(0, N - 1)])
+    blocks = nn(by_block, fg_ref[...].reshape(512, 128)).astype(BF).reshape(B, 32, 128)
+    for h in range(2):
+        first_grad[:, h * 32 : h * 32 + 32, :] = blocks[:, :, h * 64 : h * 64 + 64]
+    stores[3].start()
 
     for kind, part in (
         (TOK, tok_all.at[0]),
         (TOK_FAR, tok_all.at[0]),
         (TOK_LAST, tok_all.at[0]),
         (FIRST, first_in.at[pl.ds(0, N - 1)]),
-        (WROW, w_rows.at[pl.ds(0, 3)]),
         (GRAD, grad_in.at[pl.ds(0, N - 1)]),
         (MIXED, first_in.at[pl.ds(0, N - 1)]),
         (BACK, first_in.at[pl.ds(0, N - 1)]),
-        (PRE, pre_all.at[0]),
-        (PRE_FAR, pre_all.at[0]),
-        (PRE_LAST, pre_all.at[0]),
+        (PAIR, pair_out),
+        (ACROSS, across_out),
         (GATE_A, gate_a_in.at[pl.ds(0, 7)]),
         (GATE_B, gate_b_in.at[pl.ds(0, 7)]),
         (GATE_A2, gate_a2_in.at[pl.ds(0, 7)]),
@@ -357,30 +395,52 @@
         (ST_ALL, st_ref.at[pl.ds(0, 63)]),
     ):
         sent(kind, part)
+    for store in stores:
+        store.wait()
+
+
+def copies(*refs):
+    sources, results, held = refs[0:6], refs[6:12], refs[12:18]
+    load_sem, store_sem = refs[18:20]
+    loads = [pltpu.make_async_copy(sources[n], held[n], load_sem.at[n]) for n in range(6)]
+    stores = [pltpu.make_async_copy(held[n], results[n], store_sem.at[n]) for n in range(6)]
+    for load in loads:
+        load.start()
+    for load, store in zip(loads, stores):
+        load.wait()
+        store.start()
+    for store in stores:
+        store.wait()
 
 
 def on_device(tokens, cotangent, first_factor, second_factor, third_factor, gate_weight):
-    whole = pl.BlockSpec(memory_space=pltpu.VMEM)
     vm = pltpu.VMEM
-    output, input_grad, gate_grad, fg, st = pl.pallas_call(
+    anywhere = pl.BlockSpec(memory_space=pl.ANY)
+    shapes = (
+        jax.ShapeDtypeStruct((256, 256), BF),
+        jax.ShapeDtypeStruct((256, 256), BF),
+        jax.ShapeDtypeStruct((8, 256), F32),
+        jax.ShapeDtypeStruct((B, C, C), BF),
+        jax.ShapeDtypeStruct((B, B, C), BF),
+        jax.ShapeDtypeStruct((A, A, C), BF),
+    )
+    results = pl.pallas_call(
         kernel,
-        out_shape=(
-            jax.ShapeDtypeStruct((256, 256), BF),
-            jax.ShapeDtypeStruct((256, 256), BF),
-            jax.ShapeDtypeStruct((8, 256), F32),
-            jax.ShapeDtypeStruct((N, 4, 128), BF),
-            jax.ShapeDtypeStruct((C, 16, 128), BF),
-        ),
-        in_specs=[pl.BlockSpec(memory_space=pl.ANY)] * 6,
-        out_specs=[whole] * 5,
+        out_shape=shapes,
+        in_specs=[anywhere] * 6,
+        out_specs=[anywhere] * 6,
         scratch_shapes=[
+            *[vm(shape.shape, shape.dtype) for shape in shapes],
             vm((256, 256), BF),
             vm((256, 256), BF),
             vm((B, C, C), BF),
             vm((B, B, C), BF),
             vm((A, A, C), BF),
             vm((1024, 256), BF),
-            *[vm((4, 256, 256), BF)] * 4,
+            *[vm((4, 256, 256), BF)] * 2,
+            *[vm((2, 256, 256), BF)] * 2,
+            *[vm((256, 256), BF)] * 2,
+            vm((2, 256, 256), F32),
             vm((2, C, 4, 128), BF),
             vm((N, 4, 128), BF),
             vm((2, C, 4, 128), BF),
@@ -399,11 +459,15 @@
             vm((32, 4, 128), F32),
             vm((4, 4, 128), F32),
             vm((4, 128), BF),
+            vm((N, 4, 128), BF),
             vm((2, 16, 128), F32),
             vm((4, 16, 128), F32),
             vm((16, 128), BF),
-            pltpu.SemaphoreType.DMA((22,)),
-            pltpu.SemaphoreType.DMA((22,)),
+            vm((C, 16, 128), BF),
+            vm((16, C, 128), BF),
+            pltpu.SemaphoreType.DMA((20,)),
+            pltpu.SemaphoreType.DMA((20,)),
+            pltpu.SemaphoreType.DMA((6,)),
             pltpu.SemaphoreType.DMA((6,)),
             pltpu.SemaphoreType.REGULAR,
             pltpu.SemaphoreType.REGULAR,
@@ -419,10 +483,18 @@
         third_factor.transpose(1, 2, 0),
         gate_weight,
     )
-    first_grad = fg.reshape(32, 4, 4, 2, 64).transpose(1, 2, 3, 0, 4).reshape(B, C, C)
-    third_grad = st[:, 0:8].reshape(C, 8, 4, 32).transpose(0, 2, 1, 3).reshape(C, A, A)
-    second_grad = st[:, 8:16, 0:32].reshape(C, 8, 2, 16).transpose(0, 2, 1, 3).reshape(C, B, B)
-    return output, input_grad, first_grad, second_grad, third_grad, gate_grad
+    output, input_grad, gate_grad, first, second, third = pl.pallas_call(
+        copies,
+        out_shape=shapes,
+        in_specs=[anywhere] * 6,
+        out_specs=[anywhere] * 6,
+        scratch_shapes=[
+            *[vm(shape.shape, shape.dtype) for shape in shapes],
+            pltpu.SemaphoreType.DMA((6,)),
+            pltpu.SemaphoreType.DMA((6,)),
+        ],
+    )(*results)
+    return output, input_grad, first, second.transpose(2, 0, 1), third.transpose(2, 0, 1), gate_grad
 
 
 def solution(mesh):

time: 73.1 us -> 68.6 us (0.938)
  local copies, waits for them, and re-layouts: 6.21 us -> 0 us
  Pallas kernels: 66 us -> 67.5 us
    unnamed x13 -> x0, local copies, waits for them, and re-layouts: 2.59 us -> none
    transpose x3 -> x0, local copies, waits for them, and re-layouts: 2.17 us -> none  [the longest x1 0.81 us: on_device(): fg.reshape(32, 4, 4, 2, 64).transpose(1, 2, 3, 0, 4).reshape(B, C, C)]
    pallas_call x1 -> x2, Pallas kernels: 66 us -> 67.5 us  [the longest x1 65.5 us: on_device(): pl.pallas_call(kernel, out_shape=shapes, in_specs=[anywhere] * 6, out_spe...]
    slice x4 -> x0, local copies, waits for them, and re-layouts: 1.32 us -> none  [the longest x2 1.17 us: on_device(): st[:, 0:8].reshape(C, 8, 4, 32).transpose(0, 2, 1, 3).reshape(C, A, A)]
where the time goes in v4:
time: 68.6 us; the launch traced here: 68.2 us
  Pallas kernels  67.5 us (98%)
    pallas_call x1, Pallas kernels, on_device(): pl.pallas_call(kernel, out_shape=shapes, in_specs=[anywhere] * 6, out_spe...  65.5 us
    pallas_call x1, Pallas kernels, on_device(): pl.pallas_call(copies, out_shape=shapes, in_specs=[anywhere] * 6, out_spe...  2.02 us

profile of v4, /device:TPU:1, one launch (start us, length us, event | category | flops | bytes accessed | tf_op | source)
XLA Modules:
  0.0 68.2 jit_solution(14719274787215618705)
XLA Ops:
  0.6 65.5 %shard_map.109 = (bf16[256,256]{1,0:T(8,128)(2,1)}, bf16[256,256]{1,0:T(8,128)(2,1)}, f32[8,256]{1,0:T(8,128)}, bf16[16,64,64]{2,1,0:T(8,128)(2,1)}, bf16[16,16,...) custom-call(bf16[256,256]{1,0:T(8,128)(2,1)} %tok_hbm.1, bf16[256,256]{1,0:T(8,128)(2,1)} %cot_hbm.1, ...), custom_call_target="tpu_custom_call" | custom-call | tf_op jit(solution)/shard_map/pallas_call | solution.py:427
  66.2 2.0 %shard_map.110 = (bf16[256,256]{1,0:T(8,128)(2,1)}, bf16[256,256]{1,0:T(8,128)(2,1)}, f32[8,256]{1,0:T(8,128)}, bf16[16,64,64]{2,1,0:T(8,128)(2,1)}, bf16[16,16,...) custom-call(bf16[256,256]{1,0:T(8,128)(2,1)} %get-tuple-element.18.refs_0_, bf16[256,256]{1,0:T(8,128)(2,1)} %get-tuple-element.19.refs_1_, ...), custom_call_target="tpu_custom_call" | custom-call | tf_op jit(solution)/shard_map/pallas_call | solution.py:486

commit v5 on v4

--- a/solution.py
+++ b/solution.py
@@ -172,32 +172,30 @@
     def spread_second(t):
         return jnp.where(same_a, nt(t.astype(BF), rows16), 0.0).astype(BF)
 
+    def w_rows(p):
+        return w_ref[pl.ds(pl.multiple_of(p * 256, 256), 256), :]
+
+    def gate_term(p):
+        return nn(tok_all[p], w_rows(p))
+
+    pl.semaphore_wait(barrier, 18)
+
+    share(TOK, tok_all)
+    for d in range(1, 8):
+        greet(y_sem, {"seq_1": lax.rem(at_y + d, 8)})
     loads[2].wait()
     own_second = own(second_ref, B)
     second_mat = spread_second(nn(rows16, own_second))
     second_back = spread_second(nt(rows16, own_second))
+    pl.semaphore_wait(y_sem, 7)
+    greet(x_sem, {"seq_2": 1 - half})
     loads[3].wait()
     own_third = own(third_ref, A)
     third_mat, third_back = spread_third(nn(rows32, own_third)), spread_third(nt(rows32, own_third))
     loads[4].wait()
     upstream = nn(to_far, cot_ref[...])
     loads[5].wait()
-
-    def w_rows(p):
-        return w_ref[pl.ds(pl.multiple_of(p * 256, 256), 256), :]
-
-    def gate_term(p):
-        return nn(tok_all[p], w_rows(p))
-
     gate = gate_term(ch)
-
-    pl.semaphore_wait(barrier, 18)
-
-    share(TOK, tok_all)
-    for d in range(1, 8):
-        greet(y_sem, {"seq_1": lax.rem(at_y + d, 8)})
-    pl.semaphore_wait(y_sem, 7)
-    greet(x_sem, {"seq_2": 1 - half})
     pl.semaphore_wait(x_sem, 1)
 
     def first_for(peer):

time: 68.6 us -> 67.4 us (0.983)
  Pallas kernels: 67.5 us -> 66.6 us
    pallas_call x1, Pallas kernels: 65.5 us -> 64.6 us  [on_device(): pl.pallas_call(kernel, out_shape=shapes, in_specs=[anywhere] * 6, out_spe...]
where the time goes in v5:
time: 67.4 us; the launch traced here: 67.2 us
  Pallas kernels  66.6 us (99%)
    pallas_call x1, Pallas kernels, on_device(): pl.pallas_call(kernel, out_shape=shapes, in_specs=[anywhere] * 6, out_spe...  64.6 us
    pallas_call x1, Pallas kernels, on_device(): pl.pallas_call(copies, out_shape=shapes, in_specs=[anywhere] * 6, out_spe...  2.02 us

profile of v5, /device:TPU:1, one launch (start us, length us, event | category | flops | bytes accessed | tf_op | source)
XLA Modules:
  0.0 67.2 jit_solution(11458603188776367303)
XLA Ops:
  0.6 64.6 %shard_map.109 = (bf16[256,256]{1,0:T(8,128)(2,1)}, bf16[256,256]{1,0:T(8,128)(2,1)}, f32[8,256]{1,0:T(8,128)}, bf16[16,64,64]{2,1,0:T(8,128)(2,1)}, bf16[16,16,...) custom-call(bf16[256,256]{1,0:T(8,128)(2,1)} %tok_hbm.1, bf16[256,256]{1,0:T(8,128)(2,1)} %cot_hbm.1, ...), custom_call_target="tpu_custom_call" | custom-call | tf_op jit(solution)/shard_map/pallas_call | solution.py:425
  65.2 2.0 %shard_map.110 = (bf16[256,256]{1,0:T(8,128)(2,1)}, bf16[256,256]{1,0:T(8,128)(2,1)}, f32[8,256]{1,0:T(8,128)}, bf16[16,64,64]{2,1,0:T(8,128)(2,1)}, bf16[16,16,...) custom-call(bf16[256,256]{1,0:T(8,128)(2,1)} %get-tuple-element.18.refs_0_, bf16[256,256]{1,0:T(8,128)(2,1)} %get-tuple-element.19.refs_1_, ...), custom_call_target="tpu_custom_call" | custom-call | tf_op jit(solution)/shard_map/pallas_call | solution.py:484
